TPU v7x, 32 devices: a whole 2x2x4 slice. The times are simulated.
32 devices in a mesh: rows: 4 (over y, x), cols: 8 (over z, core).
Axes of the slice: x: 2, y: 2, z: 4, core: 2. Of those that a mesh axis runs over, the one named last changes fastest.
Arguments:
- features: bfloat16 [16, 96, 32, 512], P(None, 'rows', 'cols'), may hold values from -6 to 6
- extent: int32 [2, 16], replicated, may hold values from 4 to 96, as said below
- cotangent: bfloat16 [3, 16, 24, 8, 512], P(None, None, 'rows', 'cols'), may hold values from -6 to 6
- wide_w: float32 [4, 4608, 512], P(None, 'cols'), may hold values from -0.09375 to 0.09375
- wide_mom: float32 [4, 4608, 512], P(None, 'cols'), may hold values from -1.5 to 1.5
- wide_avg: float32 [4, 4608, 512], P(None, 'cols'), may hold values from -0.09375 to 0.09375
- point_w: float32 [6, 512, 512], P(None, 'cols'), may hold values from -0.25 to 0.25
- point_mom: float32 [6, 512, 512], P(None, 'cols'), may hold values from -1.5 to 1.5
- point_avg: float32 [6, 512, 512], P(None, 'cols'), may hold values from -0.25 to 0.25
- norm_w: float32 [2, 10, 512], replicated, as said below
- norm_mom: float32 [2, 10, 512], replicated, may hold values from -3 to 3
- norm_avg: float32 [2, 10, 512], replicated, as said below
Outputs:
- result: bfloat16 [3, 16, 24, 8, 512], P(None, None, 'rows', 'cols')
- input_grad: float32 [16, 96, 32, 512], P(None, 'rows', 'cols')
- wide_grad: float32 [4, 4608, 512], P(None, 'cols')
- wide_mom_new: float32 [4, 4608, 512], P(None, 'cols')
- wide_new: float32 [4, 4608, 512], P(None, 'cols')
- wide_avg_new: float32 [4, 4608, 512], P(None, 'cols')
- point_grad: float32 [6, 512, 512], P(None, 'cols')
- point_mom_new: float32 [6, 512, 512], P(None, 'cols')
- point_new: float32 [6, 512, 512], P(None, 'cols')
- point_avg_new: float32 [6, 512, 512], P(None, 'cols')
- norm_grad: float32 [2, 10, 512], replicated
- norm_mom_new: float32 [2, 10, 512], replicated
- norm_new: float32 [2, 10, 512], replicated
- norm_avg_new: float32 [2, 10, 512], replicated
Inputs may be any that keep to these rules, and one draw needn't show every extreme that they name: `extent`: row 0 holds each image's valid height, row 1 its valid width, in pixels; all are multiples of 4, at least half of 96 (row 0) or of 32 (row 1); some image has the full 96 and some the full 32. `norm_w`: row 0 holds positive gains, row 1 biases. `norm_avg`: row 0 holds positive averaged gains, row 1 averaged biases.
All inputs are finite; a program needn't handle non-finite values.
Results may differ from a plain program's by a relative error of at most 0.028.
Values may be sent and summed in bfloat16 or wider, within the bound.
No kernel may reach another device: no remote copies, remote signals or barrier semaphores. Data moves between devices by JAX's collectives and lax.ppermute only.
A program may use at most 256 MiB of HBM per device.

v0:
```python
import jax
import jax.numpy as jnp
from jax import lax
from jax.sharding import PartitionSpec as P

EPSILON = 1e-05
MOMENTUM = 0.9
WEIGHT_DECAY = 0.0001
AVERAGE = 0.6
RATE_NORM = 0.4


def extended(array, sides, width):
    for axis, dim in sides:
        devices, length = (lax.axis_size(axis), array.shape[dim])
        up = [(i, (i + 1) % devices) for i in range(devices - 1)]
        down = [(j, i) for i, j in up]
        last = lax.slice_in_dim(array, length - width, length, axis=dim)
        leading = lax.slice_in_dim(array, 0, width, axis=dim)
        before = lax.ppermute(last, axis, up)
        after = lax.ppermute(leading, axis, down)
        array = jnp.concatenate([before, array, after], axis=dim)
    return array


def tile_mask(extent, row_start, col_start, tile_rows, tile_cols, factor):
    heights = extent[0] // factor
    widths = extent[1] // factor
    row_ids = row_start + jnp.arange(tile_rows, dtype=jnp.int32)
    col_ids = col_start + jnp.arange(tile_cols, dtype=jnp.int32)
    inside = (row_ids[None, :, None] < heights[:, None, None]) & (
        col_ids[None, None, :] < widths[:, None, None]
    )
    return inside.astype(jnp.float32)[..., None]


def widen(statistic):
    return statistic.reshape(statistic.shape[:-1] + (1, 1, 1) + statistic.shape[-1:])


def silu_slope(values):
    logistic = jax.nn.sigmoid(values)
    return logistic * (1.0 + values * (1.0 - logistic))


def norm_forward(values, valid_mask, pixel_count, gain_row, biases):
    summed = jnp.sum(values * valid_mask, axis=(-4, -3, -2))
    squares = jnp.sum(values * values * valid_mask, axis=(-4, -3, -2))
    summed, squares = lax.psum((summed, squares), ("rows", "cols"))
    center_val = summed / pixel_count
    spread = squares / pixel_count - center_val * center_val
    inverse = lax.rsqrt(spread + EPSILON)
    normed = (values - widen(center_val)) * widen(inverse)
    return (normed, inverse, normed * widen(gain_row) + widen(biases))


def norm_backward(upstream, normed, inverse, gain_row, valid_mask, pixel_count):
    bias_sum = jnp.sum(upstream, axis=(-4, -3, -2))
    gain_sum = jnp.sum(upstream * normed, axis=(-4, -3, -2))
    bias_sum, gain_sum = lax.psum((bias_sum, gain_sum), ("rows", "cols"))
    spread_back = upstream - widen(bias_sum / pixel_count) - normed * widen(gain_sum / pixel_count)
    return (widen(gain_row * inverse) * spread_back * valid_mask, gain_sum, bias_sum)


def mean_pool(values):
    layout = values.shape
    grouped = values.reshape(layout[:-3] + (layout[-3] // 2, 2, layout[-2] // 2, 2, layout[-1]))
    return jnp.mean(grouped, axis=(-4, -2))


def pool_back(upstream):
    layout = upstream.shape
    spread_out = jnp.broadcast_to(
        jnp.expand_dims(upstream, (-4, -2)),
        layout[:-3] + (layout[-3], 2, layout[-2], 2, layout[-1]),
    )
    return 0.25 * spread_out.reshape(layout[:-3] + (2 * layout[-3], 2 * layout[-2], layout[-1]))


def window(padded, offset, tile_rows, tile_cols):
    return padded[
        ..., offset // 3 : offset // 3 + tile_rows, offset % 3 : offset % 3 + tile_cols, :
    ]


def flipped(padded, offset, tile_rows, tile_cols):
    return padded[
        ...,
        2 - offset // 3 : 2 - offset // 3 + tile_rows,
        2 - offset % 3 : 2 - offset % 3 + tile_cols,
        :,
    ]


def taps_forward(padded, weight, pattern, tile_rows, tile_cols, channels):
    summed = None
    for offset in range(9):
        partial_value = jnp.einsum(
            pattern,
            window(padded, offset, tile_rows, tile_cols),
            weight[..., offset * channels : (offset + 1) * channels, :],
            preferred_element_type=jnp.float32,
        )
        summed = partial_value if summed is None else summed + partial_value
    return summed


def taps_input(padded, weight, pattern, tile_rows, tile_cols, channels):
    summed = None
    for offset in range(9):
        partial_value = jnp.einsum(
            pattern,
            flipped(padded, offset, tile_rows, tile_cols),
            weight[..., offset * channels : (offset + 1) * channels, :],
            preferred_element_type=jnp.float32,
        )
        summed = partial_value if summed is None else summed + partial_value
    return summed


def taps_weight(padded, upstream, pattern, tile_rows, tile_cols):
    return jnp.concatenate(
        [
            jnp.einsum(
                pattern,
                window(padded, offset, tile_rows, tile_cols),
                upstream,
                preferred_element_type=jnp.float32,
            )
            for offset in range(9)
        ],
        axis=-2,
    )


def refresh(weight, gradient, moment, average, step_rate):
    descent = gradient + WEIGHT_DECAY * weight
    mom_new = MOMENTUM * moment + descent
    weight_new = weight - step_rate * (descent + MOMENTUM * mom_new)
    avg_new = AVERAGE * average + (1.0 - AVERAGE) * weight_new
    return (mom_new, weight_new, avg_new)


def shards(
    features,
    extent,
    cotangent,
    wide_w,
    wide_mom,
    wide_avg,
    point_w,
    point_mom,
    point_avg,
    norm_w,
    norm_mom,
    norm_avg,
):
    task_count = point_w.shape[0] // 2
    channels = features.shape[-1]
    rate_wide = 0.4 / (9.0 * channels) ** 0.5
    rate_point = 2.0 / float(channels) ** 0.5
    tile_rows, tile_cols = (features.shape[1], features.shape[2])
    half_rows, half_cols = (tile_rows // 2, tile_cols // 2)
    row_index = lax.axis_index("rows")
    col_index = lax.axis_index("cols")
    full_mask = tile_mask(
        extent, row_index * tile_rows, col_index * tile_cols, tile_rows, tile_cols, 1
    )
    half_mask = tile_mask(
        extent, row_index * half_rows, col_index * half_cols, half_rows, half_cols, 2
    )
    full_count = jnp.sum(extent[0] * extent[1]).astype(jnp.float32)
    half_count = full_count / 4.0
    gain_rows = norm_w[0, 1:].reshape(task_count, 3, channels)
    biases = norm_w[1, 1:].reshape(task_count, 3, channels)
    shared_w = lax.all_gather(wide_w[:1].astype(jnp.bfloat16), "cols", axis=1, tiled=True)[0]
    masked_input = features * full_mask.astype(jnp.bfloat16)
    input_padded = extended(masked_input, (("rows", 1), ("cols", 2)), 1)
    shared = taps_forward(input_padded, shared_w, "bhwc,cd->bhwd", tile_rows, tile_cols, channels)
    normed_shared, inverse_shared, linear_shared = norm_forward(
        shared, full_mask, full_count, norm_w[0, 0], norm_w[1, 0]
    )
    lifted = jax.nn.silu(linear_shared) * full_mask
    pooled = mean_pool(lifted).astype(jnp.bfloat16)
    branch_w, point_full = (
        lax.all_gather(wide_w[1:].astype(jnp.bfloat16), "cols", axis=1, tiled=True),
        lax.all_gather(point_w.astype(jnp.bfloat16), "cols", axis=1, tiled=True),
    )
    first_proj = jnp.einsum(
        "bhwc,tcd->tbhwd", pooled, point_full[:task_count], preferred_element_type=jnp.float32
    )
    normed_first, inverse_first, linear_first = norm_forward(
        first_proj, half_mask, half_count, gain_rows[:, 0], biases[:, 0]
    )
    hidden = (jax.nn.silu(linear_first) * half_mask).astype(jnp.bfloat16)
    second = jnp.einsum(
        "tbhwc,tcd->tbhwd", hidden, point_full[task_count:], preferred_element_type=jnp.float32
    )
    normed_second, inverse_second, linear_second = norm_forward(
        second, half_mask, half_count, gain_rows[:, 1], biases[:, 1]
    )
    attention = jax.nn.sigmoid(linear_second)
    pooled_wide = pooled.astype(jnp.float32)
    masked = (attention * pooled_wide).astype(jnp.bfloat16)
    masked_padded = extended(masked, (("rows", 2), ("cols", 3)), 1)
    branch = taps_forward(
        masked_padded, branch_w, "tbhwc,tcd->tbhwd", half_rows, half_cols, channels
    )
    normed_third, inverse_third, linear_third = norm_forward(
        branch, half_mask, half_count, gain_rows[:, 2], biases[:, 2]
    )
    active = jax.nn.silu(linear_third) * half_mask
    pooled_out = mean_pool(active)
    scaled = cotangent.astype(jnp.float32) * lax.rsqrt(full_count / 16.0)
    grad_active = pool_back(scaled) * silu_slope(linear_third) * half_mask
    grad_branch, gain_third, bias_third = norm_backward(
        grad_active, normed_third, inverse_third, gain_rows[:, 2], half_mask, half_count
    )
    branch_low = grad_branch.astype(jnp.bfloat16)
    branch_grad = taps_weight(masked_padded, branch_low, "tbhwc,tbhwd->tcd", half_rows, half_cols)
    branch_padded = extended(branch_low, (("rows", 2), ("cols", 3)), 1)
    grad_masked = taps_input(
        branch_padded, branch_w, "tbhwd,tcd->tbhwc", half_rows, half_cols, channels
    )
    grad_attention = grad_masked * pooled_wide * attention * (1.0 - attention)
    grad_second, gain_second, bias_second = norm_backward(
        grad_attention, normed_second, inverse_second, gain_rows[:, 1], half_mask, half_count
    )
    second_low = grad_second.astype(jnp.bfloat16)
    second_grad = jnp.einsum(
        "tbhwc,tbhwd->tcd", hidden, second_low, preferred_element_type=jnp.float32
    )
    grad_hidden = jnp.einsum(
        "tbhwd,tcd->tbhwc", second_low, point_full[task_count:], preferred_element_type=jnp.float32
    )
    grad_linear = grad_hidden * silu_slope(linear_first) * half_mask
    grad_first, gain_first, bias_first = norm_backward(
        grad_linear, normed_first, inverse_first, gain_rows[:, 0], half_mask, half_count
    )
    first_low = grad_first.astype(jnp.bfloat16)
    first_grad = jnp.einsum(
        "bhwc,tbhwd->tcd", pooled, first_low, preferred_element_type=jnp.float32
    )
    point_local = jnp.concatenate([first_grad, second_grad], axis=0)
    grad_pooled = jnp.einsum(
        "tbhwd,tcd->bhwc", first_low, point_full[:task_count], preferred_element_type=jnp.float32
    ) + jnp.sum(grad_masked * attention, axis=0)
    grad_lifted = pool_back(grad_pooled) * silu_slope(linear_shared) * full_mask
    grad_shared, gain_shared, bias_shared = norm_backward(
        grad_lifted, normed_shared, inverse_shared, norm_w[0, 0], full_mask, full_count
    )
    shared_low = grad_shared.astype(jnp.bfloat16)
    shared_grad = taps_weight(input_padded, shared_low, "bhwc,bhwd->cd", tile_rows, tile_cols)
    shared_padded = extended(shared_low, (("rows", 1), ("cols", 2)), 1)
    input_grad = (
        taps_input(shared_padded, shared_w, "bhwd,cd->bhwc", tile_rows, tile_cols, channels)
        * full_mask
    )
    wide_local = jnp.concatenate([shared_grad[None], branch_grad], axis=0)
    wide_share, point_share = (
        lax.psum_scatter(
            wide_local.astype(jnp.bfloat16), "cols", scatter_dimension=1, tiled=True
        ).astype(jnp.float32),
        lax.psum_scatter(
            point_local.astype(jnp.bfloat16), "cols", scatter_dimension=1, tiled=True
        ).astype(jnp.float32),
    )
    wide_share, point_share = (
        lax.psum(wide_share.astype(jnp.bfloat16), "rows").astype(jnp.float32),
        lax.psum(point_share.astype(jnp.bfloat16), "rows").astype(jnp.float32),
    )
    gain_grad = jnp.concatenate(
        [
            gain_shared[None],
            jnp.stack([gain_first, gain_second, gain_third], axis=1).reshape(
                3 * task_count, channels
            ),
        ],
        axis=0,
    )
    bias_grad = jnp.concatenate(
        [
            bias_shared[None],
            jnp.stack([bias_first, bias_second, bias_third], axis=1).reshape(
                3 * task_count, channels
            ),
        ],
        axis=0,
    )
    norm_grad = jnp.stack([gain_grad, bias_grad])
    wide_mom_new, wide_new, wide_avg_new = refresh(
        wide_w, wide_share, wide_mom, wide_avg, rate_wide
    )
    point_mom_new, point_new, point_avg_new = refresh(
        point_w, point_share, point_mom, point_avg, rate_point
    )
    norm_mom_new, norm_new, norm_avg_new = refresh(norm_w, norm_grad, norm_mom, norm_avg, RATE_NORM)
    return (
        pooled_out.astype(jnp.bfloat16),
        input_grad,
        wide_share,
        wide_mom_new,
        wide_new,
        wide_avg_new,
        point_share,
        point_mom_new,
        point_new,
        point_avg_new,
        norm_grad,
        norm_mom_new,
        norm_new,
        norm_avg_new,
    )


def solution(mesh):
    placed = (
        P(None, "rows", "cols", None),
        P(),
        P(None, None, "rows", "cols", None),
        P(None, "cols", None),
        P(None, "cols", None),
        P(None, "cols", None),
        P(None, "cols", None),
        P(None, "cols", None),
        P(None, "cols", None),
        P(),
        P(),
        P(),
    )
    return jax.shard_map(
        shards,
        mesh=mesh,
        in_specs=placed,
        out_specs=(
            P(None, None, "rows", "cols", None),
            P(None, "rows", "cols", None),
            P(None, "cols", None),
            P(None, "cols", None),
            P(None, "cols", None),
            P(None, "cols", None),
            P(None, "cols", None),
            P(None, "cols", None),
            P(None, "cols", None),
            P(None, "cols", None),
            P(),
            P(),
            P(),
            P(),
        ),
        check_vma=False,
    )
```

profile of v0, /device:TPU:0, one launch (start us, length us, event | category | flops | bytes accessed | tf_op | source)
XLA Modules:
  0.0 925.2 jit_solution(13083583657546032585)
XLA Ops:
  15.1 4.8 collective-permute-start
  38.2 32.5 %all-gather.4.cloned.1.call-done = bf16[1,4608,512]{2,1,0:T(8,128)(2,1)} async-done(((bf16[1,576,512]{2,1,0:T(8,128)(2,1)}), bf16[1,4608,512]{2,1,0:T(8,128)(2,1)}) %all-gather.4.cloned.1.call-update) | async-done | bytes 4718608 | tf_op jit(solution)/shard_map/all_gather | solution.py:176
  87.0 5.7 multiply_reduce_fusion.2
  92.8 39.3 %all-reduce.7 = (f32[512]{0:T(512)S(1)}, f32[512]{0:T(512)S(1)}) all-reduce(f32[512]{0:T(512)S(1)} %get-tuple-element.73, f32[512]{0:T(512)S(1)} %get-tuple-element.72), channel_id=1, replica_groups=mesh['rows'=4,'cols'=8] {'rows','cols'}, use_global_device_ids=true, to_apply=%region_4.5 | all-reduce | flops 1024 | bytes 8192 | tf_op jit(solution)/shard_map/psum | solution.py:49
  135.4 5.2 reshape.340
  150.2 44.4 %all-reduce.6 = (f32[3,512]{1,0:T(4,128)S(1)}, f32[3,512]{1,0:T(4,128)S(1)}) all-reduce(f32[3,512]{1,0:T(4,128)S(1)} %get-tuple-element.84, f32[3,512]{1,0:T(4,128)S(1)} %get-tuple-element.83), channel_id=1, replica_groups=mesh['rows'=4,'cols'=8] {'rows','cols'}, use_global_device_ids=true, to_apply=%region_9.10 | all-reduce | flops 3072 | bytes 24576 | tf_op jit(solution)/shard_map/psum | solution.py:49
  198.8 46.1 %all-reduce.5 = (f32[3,512]{1,0:T(4,128)S(1)}, f32[3,512]{1,0:T(4,128)S(1)}) all-reduce(f32[3,512]{1,0:T(4,128)S(1)} %get-tuple-element.82, f32[3,512]{1,0:T(4,128)S(1)} %get-tuple-element.81), channel_id=1, replica_groups=mesh['rows'=4,'cols'=8] {'rows','cols'}, use_global_device_ids=true, to_apply=%region_13.14 | all-reduce | flops 3072 | bytes 24576 | tf_op jit(solution)/shard_map/psum | solution.py:49
  253.9 4.5 collective-permute-done.5
  280.8 48.2 %all-reduce.4 = (f32[3,512]{1,0:T(4,128)}, f32[3,512]{1,0:T(4,128)}) all-reduce(f32[3,512]{1,0:T(4,128)} %get-tuple-element.80, f32[3,512]{1,0:T(4,128)} %get-tuple-element.79), channel_id=1, replica_groups=mesh['rows'=4,'cols'=8] {'rows','cols'}, use_global_device_ids=true, to_apply=%region_17.18 | all-reduce | flops 3072 | bytes 24576 | tf_op jit(solution)/shard_map/psum | solution.py:49
  335.1 40.7 %all-reduce.3 = (f32[3,512]{1,0:T(4,128)}, f32[3,512]{1,0:T(4,128)}) all-reduce(f32[3,512]{1,0:T(4,128)} %get-tuple-element.71, f32[3,512]{1,0:T(4,128)} %get-tuple-element.70), channel_id=1, replica_groups=mesh['rows'=4,'cols'=8] {'rows','cols'}, use_global_device_ids=true, to_apply=%region_23.24 | all-reduce | flops 3072 | bytes 24576 | tf_op jit(solution)/shard_map/psum | solution.py:60
  381.5 5.0 collective-permute-start.8
  401.3 4.4 slice-done.10
  428.3 8.4 multiply_reduce_fusion.4
  436.7 42.2 %all-reduce.2 = (f32[3,512]{1,0:T(4,128)S(1)}, f32[3,512]{1,0:T(4,128)S(1)}) all-reduce(f32[3,512]{1,0:T(4,128)S(1)} %get-tuple-element.77, f32[3,512]{1,0:T(4,128)S(1)} %get-tuple-element.87), channel_id=1, replica_groups=mesh['rows'=4,'cols'=8] {'rows','cols'}, use_global_device_ids=true, to_apply=%region_27.28 | all-reduce | flops 3072 | bytes 24576 | tf_op jit(solution)/shard_map/psum | solution.py:60
  487.3 40.0 %all-reduce.1 = (f32[3,512]{1,0:T(4,128)S(1)}, f32[3,512]{1,0:T(4,128)S(1)}) all-reduce(f32[3,512]{1,0:T(4,128)S(1)} %get-tuple-element.86, f32[3,512]{1,0:T(4,128)S(1)} %get-tuple-element.85), channel_id=1, replica_groups=mesh['rows'=4,'cols'=8] {'rows','cols'}, use_global_device_ids=true, to_apply=%region_31.32 | all-reduce | flops 3072 | bytes 24576 | tf_op jit(solution)/shard_map/psum | solution.py:60
  534.4 5.5 copy.317
  544.3 5.4 mul.603
  554.2 42.4 %all-reduce = (f32[512]{0:T(512)S(1)}, f32[512]{0:T(512)S(1)}) all-reduce(f32[512]{0:T(512)S(1)} %get-tuple-element.75, f32[512]{0:T(512)S(1)} %get-tuple-element.74), channel_id=1, replica_groups=mesh['rows'=4,'cols'=8] {'rows','cols'}, use_global_device_ids=true, to_apply=%region_36.37 | all-reduce | flops 1024 | bytes 8192 | tf_op jit(solution)/shard_map/psum | solution.py:60
  614.0 7.6 pad_maximum_fusion
  625.4 4.8 collective-permute-start.12
  652.1 163.2 %reduce-scatter.3.cloned.1.call-done = bf16[4,576,512]{2,1,0:T(8,128)(2,1)} async-done(((bf16[4,4608,512]{2,1,0:T(8,128)(2,1)}), bf16[4,576,512]{2,1,0:T(8,128)(2,1)}) %reduce-scatter.3.cloned.1.call-update) | async-done | bytes 2359312 | tf_op jit(solution)/shard_map/reduce_scatter | solution.py:261
  831.3 5.9 add_multiply_fusion
  841.0 58.7 %all-reduce.11.cloned.1.call-done = (bf16[6,64,512]{2,0,1:T(8,128)(2,1)}, bf16[4,576,512]{2,1,0:T(8,128)(2,1)}) async-done(((bf16[6,64,512]{2,0,1:T(8,128)(2,1)}, bf16[4,576,512]{2,1,0:T(8,128)(2,1)}), (bf16[6,64,512]{2,0,1:T(8,128)(2,1)}, bf16[4,576,512]{2,1,0:T(8,128)(2,1)})) %all-reduce.11.cloned.1.call-update) | async-done | bytes 2752528 | tf_op jit(solution)/shard_map/psum | solution.py:270
  908.9 9.2 multiply_add_fusion
  (395 shorter events, 234.4 us)
Async XLA Ops:
  7.2 63.6 %all-gather.4.cloned.1.call-start = ((), (), s32[]{:S(2)}) async-start(), calls=%async_computation.2 | async-start | bytes 5308416 | tf_op jit(solution)/shard_map/all_gather | solution.py:176
  10.8 135.6 %all-gather.6.cloned.1.call-start = ((), (), s32[]{:S(2)}) async-start(), calls=%async_computation.3 | async-start | bytes 3538944 | tf_op jit(solution)/shard_map/all_gather | solution.py:187
  11.7 253.0 %all-gather.8.cloned.1.call-start = ((), (), s32[]{:S(2)}) async-start(), calls=%async_computation.4 | async-start | bytes 15925248 | tf_op jit(solution)/shard_map/all_gather | solution.py:186
  13.1 639.0 %reduce-scatter.5.cloned.1.call-start = ((), (), s32[]{:S(2)}) async-start(), calls=%async_computation.6 | async-start | bytes 4718592 | tf_op jit(solution)/shard_map/reduce_scatter | solution.py:264
  15.1 10.2 %collective-permute-start = (bf16[16,1,4,512]{3,1,2,0:T(2,128)(2,1)S(1)}, bf16[16,1,4,512]{3,1,2,0:T(2,128)(2,1)S(1)}, u32[]{:S(2)}, u32[]{:S(2)}) collective-permute-start(bf16[16,1,4,512]{3,1,2,0:T(2,128)(2,1)S(1)} %get-tuple-element.139), channel_id=1, source_target_pairs={{0,8},{8,16},{16,24},{1,9},{9,17},{17,25},{2,10},{10,18},{18,26},{... | collective-permute-start | bytes 196616 | tf_op jit(solution)/shard_map/ppermute | solution.py:20
  19.9 7.5 collective-permute-start.1
  23.3 171.9 %copy-start.80 = (f32[3,1,512]{2,0,1:T(4,128)}, f32[3,1,512]{2,0,1:T(4,128)S(1)}, u32[]{:S(2)}) copy-start(f32[3,1,512]{2,0,1:T(4,128)S(1)} %copy.492) | copy-start | bytes 18436
  24.5 170.7 %copy-start.82 = (f32[3,1,512]{2,0,1:T(4,128)}, f32[3,1,512]{2,0,1:T(4,128)S(1)}, u32[]{:S(2)}) copy-start(f32[3,1,512]{2,0,1:T(4,128)S(1)} %copy.496) | copy-start | bytes 18436
  28.1 4.6 collective-permute-start.3
  29.4 4.6 collective-permute-start.2
  247.5 6.4 collective-permute-start.4
  251.7 6.6 collective-permute-start.5
  258.6 6.0 collective-permute-start.6
  263.0 9.9 %collective-permute-start.7 = (bf16[3,16,14,1,512]{4,1,0,3,2:T(8,128)(2,1)S(1)}, bf16[3,16,14,1,512]{4,1,0,3,2:T(8,128)(2,1)S(1)}, u32[]{:S(2)}, u32[]{:S(2)}) collective-permute-start(bf16[3,16,14,1,512]{4,1,0,3,2:T(8,128)(2,1)S(1)} %get-tuple-element.143), channel_id=1, source_target_pairs={{1,0},{2,1},{3,2},{4,3},{5,4},{6,5},{7,6},{9,8},{10,9},{11,10},{12... | collective-permute-start | bytes 2064392 | tf_op jit(solution)/shard_map/ppermute | solution.py:21
  380.2 18.9 %collective-permute-start.9 = (bf16[3,16,1,2,512]{4,1,0,3,2:T(8,128)(2,1)S(1)}, bf16[3,16,1,2,512]{4,1,0,3,2:T(8,128)(2,1)S(1)}, u32[]{:S(2)}, u32[]{:S(2)}) collective-permute-start(bf16[3,16,1,2,512]{4,1,0,3,2:T(8,128)(2,1)S(1)} %get-tuple-element.145), channel_id=1, source_target_pairs={{8,0},{16,8},{24,16},{9,1},{17,9},{25,17},{10,2},{18,10},{26,18},{... | collective-permute-start | bytes 294920 | tf_op jit(solution)/shard_map/ppermute | solution.py:21
  381.5 17.6 %collective-permute-start.8 = (bf16[3,16,1,2,512]{4,1,0,3,2:T(8,128)(2,1)S(1)}, bf16[3,16,1,2,512]{4,1,0,3,2:T(8,128)(2,1)S(1)}, u32[]{:S(2)}, u32[]{:S(2)}) collective-permute-start(bf16[3,16,1,2,512]{4,1,0,3,2:T(8,128)(2,1)S(1)} %get-tuple-element.146), channel_id=1, source_target_pairs={{0,8},{8,16},{16,24},{1,9},{9,17},{17,25},{2,10},{10,18},{18,26},{... | collective-permute-start | bytes 294920 | tf_op jit(solution)/shard_map/ppermute | solution.py:20
  399.4 16.1 %collective-permute-start.10 = (bf16[3,16,14,1,512]{4,1,0,3,2:T(8,128)(2,1)S(1)}, bf16[3,16,14,1,512]{4,1,0,3,2:T(8,128)(2,1)S(1)}, u32[]{:S(2)}, u32[]{:S(2)}) collective-permute-start(bf16[3,16,14,1,512]{4,1,0,3,2:T(8,128)(2,1)S(1)} %get-tuple-element.142), channel_id=1, source_target_pairs={{1,0},{2,1},{3,2},{4,3},{5,4},{6,5},{7,6},{9,8},{10,9},{11,10},{12... | collective-permute-start | bytes 2064392 | tf_op jit(solution)/shard_map/ppermute | solution.py:21
  409.5 12.6 %collective-permute-start.11 = (bf16[3,16,14,1,512]{4,1,0,3,2:T(8,128)(2,1)S(1)}, bf16[3,16,14,1,512]{4,1,0,3,2:T(8,128)(2,1)S(1)}, u32[]{:S(2)}, u32[]{:S(2)}) collective-permute-start(bf16[3,16,14,1,512]{4,1,0,3,2:T(8,128)(2,1)S(1)} %get-tuple-element.141), channel_id=1, source_target_pairs={{0,1},{1,2},{2,3},{3,4},{4,5},{5,6},{6,7},{8,9},{9,10},{10,11},{11... | collective-permute-start | bytes 2064392 | tf_op jit(solution)/shard_map/ppermute | solution.py:20
  539.9 275.3 %reduce-scatter.3.cloned.1.call-start = ((), (), s32[]{:S(2)}) async-start(), calls=%async_computation.5 | async-start | bytes 21233664 | tf_op jit(solution)/shard_map/reduce_scatter | solution.py:261
  621.7 278.0 %all-reduce.11.cloned.1.call-start = ((), (), s32[]{:S(2)}) async-start(), calls=%async_computation.7 | async-start | bytes 5767168 | tf_op jit(solution)/shard_map/psum | solution.py:270
  624.1 12.6 %collective-permute-start.13 = (bf16[16,1,4,512]{3,1,2,0:T(2,128)(2,1)S(1)}, bf16[16,1,4,512]{3,1,2,0:T(2,128)(2,1)S(1)}, u32[]{:S(2)}, u32[]{:S(2)}) collective-permute-start(bf16[16,1,4,512]{3,1,2,0:T(2,128)(2,1)S(1)} %get-tuple-element.137), channel_id=1, source_target_pairs={{8,0},{16,8},{24,16},{9,1},{17,9},{25,17},{10,2},{18,10},{26,18},{... | collective-permute-start | bytes 196616 | tf_op jit(solution)/shard_map/ppermute | solution.py:21
  625.4 11.3 %collective-permute-start.12 = (bf16[16,1,4,512]{3,1,2,0:T(2,128)(2,1)S(1)}, bf16[16,1,4,512]{3,1,2,0:T(2,128)(2,1)S(1)}, u32[]{:S(2)}, u32[]{:S(2)}) collective-permute-start(bf16[16,1,4,512]{3,1,2,0:T(2,128)(2,1)S(1)} %get-tuple-element.138), channel_id=1, source_target_pairs={{0,8},{8,16},{16,24},{1,9},{9,17},{17,25},{2,10},{10,18},{18,26},{... | collective-permute-start | bytes 196616 | tf_op jit(solution)/shard_map/ppermute | solution.py:20
  637.4 10.3 %collective-permute-start.15 = (bf16[16,26,1,512]{3,1,2,0:T(8,128)(2,1)S(1)}, bf16[16,26,1,512]{3,1,2,0:T(8,128)(2,1)S(1)}, u32[]{:S(2)}, u32[]{:S(2)}) collective-permute-start(bf16[16,26,1,512]{3,1,2,0:T(8,128)(2,1)S(1)} %get-tuple-element.131), channel_id=1, source_target_pairs={{0,1},{1,2},{2,3},{3,4},{4,5},{5,6},{6,7},{8,9},{9,10},{10,11},{11... | collective-permute-start | bytes 1277960 | tf_op jit(solution)/shard_map/ppermute | solution.py:20
  638.7 9.0 collective-permute-start.14
  (100 other events, 1545.4 us)
Sparse Core Ops, SparseCore 0:
  10.9 59.7 all-gather.3
  72.9 37.1 all-gather.5
  112.3 130.6 all-gather.7
  540.0 51.4 reduce-scatter.4
  621.8 193.3 reduce-scatter.2
  818.3 81.3 all-reduce.10
where the time goes:
time: 930 us; the launch traced here: 925 us
  blocking collectives  343 us (37%)
  waiting for transfers between devices  263 us (28%)
  matrix products  131 us (14%)
  other arithmetic  70.8 us (8%)
  local copies, waits for them, and re-layouts  61.9 us (7%)
  starting transfers between devices  38.6 us (4%)
  between operations  16.7 us (2%)
    psum x4, blocking collectives, norm_forward(): summed, squares = lax.psum((summed, squares), ('rows', 'cols'))  178 us
    psum x4, blocking collectives, norm_backward(): bias_sum, gain_sum = lax.psum((bias_sum, gain_sum), ('rows', 'cols'))  165 us
    reduce_scatter x1, waiting for transfers between devices, shards(): lax.psum_scatter(wide_local.astype(jnp.bfloat16), 'cols', scatter_dimensi...  163 us
    dot_general x18, matrix products, taps_input(): jnp.einsum(pattern, flipped(padded, offset, tile_rows, tile_cols), weight...  59.5 us
    psum x1, waiting for transfers between devices, shards(): lax.psum(point_share.astype(jnp.bfloat16), 'rows').astype(jnp.float32)  58.7 us
    unnamed x219, local copies, waits for them, and re-layouts  34.8 us
    dot_general x18, matrix products, taps_forward(): jnp.einsum(pattern, window(padded, offset, tile_rows, tile_cols), weight[...  34.7 us
    all_gather x1, waiting for transfers between devices, shards(): lax.all_gather(wide_w[:1].astype(jnp.bfloat16), 'cols', axis=1, tiled=True)  32.5 us
  transfers between devices with their start and end apart: 22, of which 7 were waited for; matrix products, arithmetic and copies ran while one was open for 18% of the time, Pallas kernels for 0%

commit v1 on v0

v1 whole, which is shorter than its diff:
```python
import functools

import jax
import jax.numpy as jnp
from jax import lax
from jax.experimental import pallas as pl
from jax.experimental.pallas import tpu as pltpu
from jax.sharding import Mesh
from jax.sharding import PartitionSpec as P

EPSILON = 1e-05
MOMENTUM = 0.9
WEIGHT_DECAY = 0.0001
AVERAGE = 0.6
RATE_NORM = 0.4
F32 = jnp.float32
BF16 = jnp.bfloat16
EVERY = ("rows", "chips", "core")
PAIR = [(0, 1), (1, 0)]
VMEM_LIMIT = 56 * 1024 * 1024


def sigmoid(values):
    return 0.5 * jnp.tanh(0.5 * values) + 0.5


def flat(values):
    return values.reshape((-1, values.shape[-1]))


def mask_of(ext_ref, row, col, rows, cols):
    shape = (rows, cols) + ext_ref.shape[1:]
    row_ids = row + lax.broadcasted_iota(jnp.int32, shape, 0)
    col_ids = col + lax.broadcasted_iota(jnp.int32, shape, 1)
    inside = (row_ids < ext_ref[0][None, None]) & (col_ids < ext_ref[1][None, None])
    return inside


def keep(inside, values):
    return jnp.where(inside, values, 0.0)


def sums_of(first, second):
    return jnp.concatenate(
        [jnp.sum(flat(first), axis=0, keepdims=True), jnp.sum(flat(second), axis=0, keepdims=True)],
        axis=0,
    )


def moments(total, inv_count):
    center = total[0:1] * inv_count
    spread = total[1:2] * inv_count - center * center
    return center, lax.rsqrt(spread + EPSILON)


def taps_dot(source, weight, rows, cols, row, mirrored):
    channels = weight.shape[-1]
    total = None
    for tap in range(9):
        dr, dc = tap // 3, tap % 3
        if mirrored:
            dr, dc = 2 - dr, 2 - dc
        window = flat(source[pl.ds(row + dr, rows), dc : dc + cols])
        block = weight[tap * channels : (tap + 1) * channels, :]
        dims = (((1,), (1,)), ((), ())) if mirrored else (((1,), (0,)), ((), ()))
        part = lax.dot_general(window, block, dims, preferred_element_type=F32)
        total = part if total is None else total + part
    return total


def dot(left, right):
    return jnp.dot(left, right, preferred_element_type=F32)


def dot_nt(left, right):
    return lax.dot_general(left, right, (((1,), (1,)), ((), ())), preferred_element_type=F32)


def dot_tn(left, right):
    return lax.dot_general(left, right, (((0,), (0,)), ((), ())), preferred_element_type=F32)


def assemble(place_ref, pieces, w_ref, sem, task, start):
    chip, core, row = place_ref[0], place_ref[1], place_ref[2]
    half = len(pieces) // 2
    count = 0
    for side in range(2):
        own, parts = pieces[side * half], pieces[side * half + 1 : (side + 1) * half]
        depth = own.shape[1]
        width = parts[0].shape[-1]
        at_core = core if side == 0 else 1 - core

        def run(source, target, at):
            copy = pltpu.make_async_copy(source, target, sem.at[at])
            copy.start() if start else copy.wait()

        base = pl.multiple_of((2 * chip + at_core) * depth, 16)
        run(own.at[task], w_ref.at[pl.ds(base, depth)], count)
        count += 1
        for flip, part in enumerate(parts):
            lane = pl.multiple_of(jnp.bitwise_xor(row, flip) * width, 128)
            for hop in range(part.shape[0]):
                from_chip = jnp.bitwise_xor(chip, hop + 1)
                base = pl.multiple_of((2 * from_chip + at_core) * depth, 16)
                run(part.at[hop, task], w_ref.at[pl.ds(base, depth), pl.ds(lane, width)], count)
                count += 1


def gathered(place_ref, pieces, w_ref, sem):
    @pl.when(pl.program_id(0) == 0)
    def _():
        assemble(place_ref, pieces, w_ref, sem.at[0], 0, True)
        assemble(place_ref, pieces, w_ref, sem.at[0], 0, False)


def shared_fwd_kernel(rows, place_ref, x_ref, ext_ref, *refs):
    *pieces, z_ref, stat_ref, acc_ref, w_ref, sem = refs
    gathered(place_ref, pieces, w_ref, sem)
    step = pl.program_id(0)
    cols = z_ref.shape[1]
    z = taps_dot(x_ref, w_ref, rows, cols, step * rows, False).reshape(z_ref.shape)
    z_ref[...] = z
    zm = keep(mask_of(ext_ref, step * rows, 0, rows, cols), z)
    part = sums_of(zm, zm * z)

    @pl.when(step == 0)
    def _():
        acc_ref[...] = part

    @pl.when(step > 0)
    def _():
        acc_ref[...] += part

    @pl.when(step == pl.num_programs(0) - 1)
    def _():
        stat_ref[...] = jnp.broadcast_to(acc_ref[...][None], stat_ref.shape)


def pool_kernel(rows, z_ref, stat_ref, meta_ref, norm_ref, ext_ref, p_ref, out_ref, st_ref, pool_ref, aff_ref):
    step = pl.program_id(0)
    cols = z_ref.shape[1]

    @pl.when(step == 0)
    def _():
        center, inverse = moments(jnp.sum(stat_ref[...], axis=0), meta_ref[0:1])
        scale = inverse * norm_ref[0, 0:1]
        aff_ref[0:1] = scale
        aff_ref[1:2] = norm_ref[1, 0:1] - center * scale

    v = z_ref[...] * aff_ref[0:1] + aff_ref[1:2]
    lifted = keep(mask_of(ext_ref, step * rows, 0, rows, cols), v * sigmoid(v))
    grouped = lifted.reshape((rows // 2, 2, cols // 2, 2) + lifted.shape[2:])
    mean = 0.25 * (
        (grouped[:, 0, :, 0] + grouped[:, 0, :, 1]) + (grouped[:, 1, :, 0] + grouped[:, 1, :, 1])
    )
    low = mean.astype(BF16)
    out_ref[...] = low
    pool_ref[pl.ds(step * (rows // 2), rows // 2)] = low

    @pl.when(step == pl.num_programs(0) - 1)
    def _():
        left = flat(pool_ref[...])
        for task in range(p_ref.shape[0]):
            f = dot(left, p_ref[task])
            st_ref[:, task] = jnp.broadcast_to(
                sums_of(f, f * f)[None], (st_ref.shape[0],) + st_ref.shape[2:]
            )


def task_norm(stat_ref, meta_ref, norm_ref, task, slot):
    center, inverse = moments(jnp.sum(stat_ref[:, 0], axis=0), meta_ref[1:2])
    row = 1 + 3 * task + slot
    gain = norm_ref[0, pl.ds(row, 1)]
    bias = norm_ref[1, pl.ds(row, 1)]
    return center, inverse, gain, bias


def attend_kernel(pe_ref, stat_ref, meta_ref, norm_ref, ext_ref, p1_ref, p2_ref, first_ref, hidden_ref, second_ref, st_ref):
    task = pl.program_id(0)
    shape = pe_ref.shape
    rows, cols = shape[0] - 2, shape[1] - 2
    center, inverse, gain, bias = task_norm(stat_ref, meta_ref, norm_ref, task, 0)
    scale = inverse * gain
    shift = bias - center * scale
    first = dot(flat(pe_ref[...]), p1_ref[0])
    first_ref[0] = first.reshape(shape)[1 : 1 + rows, 1 : 1 + cols]
    v = first * scale + shift
    inside = mask_of(ext_ref, -1, -1, rows + 2, cols + 2)
    hidden = keep(inside, (v * sigmoid(v)).reshape(shape)).astype(BF16)
    hidden_ref[0] = hidden[1 : 1 + rows, 1 : 1 + cols]
    second = dot(flat(hidden), p2_ref[0]).reshape(shape)
    second_ref[0] = second
    own = second[1 : 1 + rows, 1 : 1 + cols]
    st_ref[:, 0] = jnp.broadcast_to(sums_of(own, own * own)[None], (st_ref.shape[0],) + st_ref.shape[2:])


def branch_fwd_kernel(second_ref, pe_ref, stat_ref, meta_ref, norm_ref, ext_ref, w_ref, masked_ref, branch_ref, st_ref):
    task = pl.program_id(0)
    rows, cols = branch_ref.shape[1:3]
    center, inverse, gain, bias = task_norm(stat_ref, meta_ref, norm_ref, task, 1)
    scale = inverse * gain
    shift = bias - center * scale
    attention = sigmoid(second_ref[0] * scale + shift)
    masked_ref[0] = (attention * pe_ref[...].astype(F32)).astype(BF16)
    z = taps_dot(masked_ref.at[0], w_ref.at[0], rows, cols, 0, False).reshape(branch_ref.shape[1:])
    branch_ref[0] = z
    zm = keep(mask_of(ext_ref, 0, 0, rows, cols), z)
    st_ref[:, 0] = jnp.broadcast_to(sums_of(zm, zm * z)[None], (st_ref.shape[0],) + st_ref.shape[2:])


def branch_grad_terms(branch_ref, cot_ref, stat_ref, meta_ref, norm_ref, ext_ref, task):
    rows, cols = branch_ref.shape[1:3]
    center, inverse, gain, bias = task_norm(stat_ref, meta_ref, norm_ref, task, 2)
    zhat = (branch_ref[0] - center) * inverse
    v = zhat * gain + bias
    s = sigmoid(v)
    inside = mask_of(ext_ref, 0, 0, rows, cols)
    c = cot_ref[0].astype(F32) * (0.25 * meta_ref[2:3])
    spread = jnp.broadcast_to(c[:, None, :, None], (rows // 2, 2, cols // 2, 2) + c.shape[2:])
    upstream = keep(inside, spread.reshape(v.shape) * (s * (1.0 + v * (1.0 - s))))
    return zhat, v, s, inside, upstream, gain * inverse


def result_kernel(branch_ref, cot_ref, stat_ref, meta_ref, norm_ref, ext_ref, out_ref, st_ref):
    task = pl.program_id(0)
    rows, cols = branch_ref.shape[1:3]
    zhat, v, s, inside, upstream, _ = branch_grad_terms(
        branch_ref, cot_ref, stat_ref, meta_ref, norm_ref, ext_ref, task
    )
    active = keep(inside, v * s)
    grouped = active.reshape((rows // 2, 2, cols // 2, 2) + active.shape[2:])
    mean = 0.25 * (
        (grouped[:, 0, :, 0] + grouped[:, 0, :, 1]) + (grouped[:, 1, :, 0] + grouped[:, 1, :, 1])
    )
    out_ref[0] = mean.astype(BF16)
    st_ref[:, 0] = jnp.broadcast_to(
        sums_of(upstream, upstream * zhat)[None], (st_ref.shape[0],) + st_ref.shape[2:]
    )


def back_sums(stat_ref, inv_count):
    total = jnp.sum(stat_ref[:, 0], axis=0)
    return total[0:1] * inv_count, total[1:2] * inv_count


def branch_dz_kernel(branch_ref, cot_ref, stat_ref, back_ref, meta_ref, norm_ref, ext_ref, dz_ref):
    task = pl.program_id(0)
    zhat, v, s, inside, upstream, factor = branch_grad_terms(
        branch_ref, cot_ref, stat_ref, meta_ref, norm_ref, ext_ref, task
    )
    bias_mean, gain_mean = back_sums(back_ref, meta_ref[1:2])
    dz_ref[0] = keep(inside, factor * (upstream - bias_mean - zhat * gain_mean)).astype(BF16)


def branch_dgrad_kernel(dz_ref, w_ref, second_ref, pooled_ref, stat_ref, meta_ref, norm_ref, ga_ref, prod_ref, st_ref):
    task = pl.program_id(0)
    shape = pooled_ref.shape
    rows, cols = shape[:2]
    center, inverse, gain, bias = task_norm(stat_ref, meta_ref, norm_ref, task, 1)
    grad = taps_dot(dz_ref.at[0], w_ref.at[0], rows, cols, 0, True).reshape(shape)
    zhat = (second_ref[0, 1 : 1 + rows, 1 : 1 + cols] - center) * inverse
    attention = sigmoid(zhat * gain + bias)
    through = grad * attention
    ga = through * pooled_ref[...].astype(F32) * (1.0 - attention)
    ga_ref[0] = ga

    @pl.when(task == 0)
    def _():
        prod_ref[...] = through

    @pl.when(task > 0)
    def _():
        prod_ref[...] += through

    st_ref[:, 0] = jnp.broadcast_to(sums_of(ga, ga * zhat)[None], (st_ref.shape[0],) + st_ref.shape[2:])


def branch_wgrad_kernel(own_ref, other_ref, dz_own_ref, dz_other_ref, out_ref):
    rows, cols = dz_own_ref.shape[1:3]
    own = flat(dz_own_ref[0])
    other = flat(dz_other_ref[0])
    for tap in range(9):
        dr, dc = tap // 3, tap % 3
        total = dot_tn(flat(own_ref[0, dr : dr + rows, dc : dc + cols]), own)
        total += dot_tn(flat(other_ref[0, dr : dr + rows, dc : dc + cols]), other)
        out_ref[0, tap] = total.astype(BF16)


def attend_back_kernel(ga_ref, second_ref, stat2_ref, back_ref, hidden_ref, p2_ref, first_ref, stat1_ref, meta_ref, norm_ref, ext_ref, wg_ref, gl_ref, st_ref):
    task = pl.program_id(0)
    shape = ga_ref.shape[1:]
    rows, cols = shape[:2]
    center, inverse, gain, _ = task_norm(stat2_ref, meta_ref, norm_ref, task, 1)
    zhat = (second_ref[0, 1 : 1 + rows, 1 : 1 + cols] - center) * inverse
    bias_mean, gain_mean = back_sums(back_ref, meta_ref[1:2])
    inside = mask_of(ext_ref, 0, 0, rows, cols)
    dz = keep(inside, gain * inverse * (ga_ref[0] - bias_mean - zhat * gain_mean)).astype(BF16)
    wg_ref[0] = dot_tn(flat(hidden_ref[0]), flat(dz)).astype(BF16)
    grad_hidden = dot_nt(flat(dz), p2_ref[0]).reshape(shape)
    center, inverse, gain, bias = task_norm(stat1_ref, meta_ref, norm_ref, task, 0)
    zhat = (first_ref[0] - center) * inverse
    v = zhat * gain + bias
    s = sigmoid(v)
    gl = keep(inside, grad_hidden * (s * (1.0 + v * (1.0 - s))))
    gl_ref[0] = gl
    st_ref[:, 0] = jnp.broadcast_to(sums_of(gl, gl * zhat)[None], (st_ref.shape[0],) + st_ref.shape[2:])


def unpool(grad, rows, cols):
    spread = jnp.broadcast_to(grad[:, None, :, None], (rows // 2, 2, cols // 2, 2) + grad.shape[2:])
    return spread.reshape((rows, cols) + grad.shape[2:])


def shared_grad_terms(z, grad, center, inverse, gain, bias, inside):
    zhat = (z - center) * inverse
    v = zhat * gain + bias
    s = sigmoid(v)
    upstream = keep(inside, unpool(0.25 * grad, z.shape[0], z.shape[1]) * (s * (1.0 + v * (1.0 - s))))
    return zhat, upstream


def pooled_back_kernel(chunk, gl_ref, first_ref, stat1_ref, back_ref, pooled_ref, p1_ref, prod_ref, z_ref, stat0_ref, meta_ref, norm_ref, ext_ref, full_ref, wg_ref, gp_ref, st_ref):
    task = pl.program_id(0)
    shape = gl_ref.shape[1:]
    rows, cols = shape[:2]
    center, inverse, gain, _ = task_norm(stat1_ref, meta_ref, norm_ref, task, 0)
    zhat = (first_ref[0] - center) * inverse
    bias_mean, gain_mean = back_sums(back_ref, meta_ref[1:2])
    inside = mask_of(ext_ref, 0, 0, rows, cols)
    dz = keep(inside, gain * inverse * (gl_ref[0] - bias_mean - zhat * gain_mean)).astype(BF16)
    wg_ref[0] = dot_tn(flat(pooled_ref[...]), flat(dz)).astype(BF16)
    grad = dot_nt(flat(dz), p1_ref[0]).reshape(shape)

    @pl.when(task == 0)
    def _():
        gp_ref[...] = prod_ref[...] + grad

    @pl.when(task > 0)
    def _():
        gp_ref[...] += grad

    @pl.when(task == pl.num_programs(0) - 1)
    def _():
        center, inverse = moments(jnp.sum(stat0_ref[...], axis=0), meta_ref[0:1])
        gain, bias = norm_ref[0, 0:1], norm_ref[1, 0:1]
        full_rows, full_cols = z_ref.shape[:2]

        def body(i, total):
            row = i * chunk
            inside = mask_of(full_ref, row, 0, chunk, full_cols)
            zhat, upstream = shared_grad_terms(
                z_ref[pl.ds(row, chunk)], gp_ref[pl.ds(i * (chunk // 2), chunk // 2)],
                center, inverse, gain, bias, inside,
            )
            return total + sums_of(upstream, upstream * zhat)

        total = lax.fori_loop(0, full_rows // chunk, body, jnp.zeros(st_ref.shape[1:], F32))
        st_ref[...] = jnp.broadcast_to(total[None], st_ref.shape)


def shared_dz_kernel(rows, z_ref, gp_ref, stat_ref, back_ref, meta_ref, norm_ref, ext_ref, dz_ref):
    step = pl.program_id(0)
    cols = z_ref.shape[1]
    center, inverse = moments(jnp.sum(stat_ref[...], axis=0), meta_ref[0:1])
    gain, bias = norm_ref[0, 0:1], norm_ref[1, 0:1]
    total = jnp.sum(back_ref[...], axis=0) * meta_ref[0:1]
    inside = mask_of(ext_ref, step * rows, 0, rows, cols)
    zhat, upstream = shared_grad_terms(z_ref[...], gp_ref[...], center, inverse, gain, bias, inside)
    dz = gain * inverse * (upstream - total[0:1] - zhat * total[1:2])
    dz_ref[...] = keep(inside, dz).astype(BF16)


def shared_wgrad_kernel(own_ref, other_ref, dz_own_ref, dz_other_ref, out_ref):
    tap = pl.program_id(0)
    rows, cols = dz_own_ref.shape[:2]
    row = tap // 3
    for dc in range(3):

        @pl.when(tap % 3 == dc)
        def _():
            total = dot_tn(flat(own_ref[pl.ds(row, rows), dc : dc + cols]), flat(dz_own_ref[...]))
            total += dot_tn(flat(other_ref[pl.ds(row, rows), dc : dc + cols]), flat(dz_other_ref[...]))
            out_ref[0] = total.astype(BF16)


def shared_dgrad_kernel(rows, place_ref, dz_ref, ext_ref, *refs):
    *pieces, out_ref, w_ref, sem = refs
    gathered(place_ref, pieces, w_ref, sem)
    step = pl.program_id(0)
    cols = out_ref.shape[1]
    grad = taps_dot(dz_ref, w_ref, rows, cols, step * rows, True).reshape(out_ref.shape)
    out_ref[...] = keep(mask_of(ext_ref, step * rows, 0, rows, cols), grad)


def whole(shape):
    return pl.BlockSpec(shape, lambda i: (0,) * len(shape))


def leading(shape):
    return pl.BlockSpec(shape, lambda i: (i,) + (0,) * (len(shape) - 1))


def second_dim(shape):
    return pl.BlockSpec(shape, lambda i: (0, i) + (0,) * (len(shape) - 2))


def call(kernel, grid, ins, outs, scratch=(), flops=0):
    arrays = [array for array, _ in ins]
    moved = sum(a.size * a.dtype.itemsize for a in arrays)
    moved += sum(s.size * s.dtype.itemsize for s, _ in outs)
    return pl.pallas_call(
        kernel,
        grid=(grid,),
        in_specs=[spec for _, spec in ins],
        out_specs=[spec for _, spec in outs],
        out_shape=[shape for shape, _ in outs],
        scratch_shapes=list(scratch),
        compiler_params=pltpu.CompilerParams(vmem_limit_bytes=VMEM_LIMIT),
        cost_estimate=pl.CostEstimate(flops=flops, bytes_accessed=moved, transcendentals=0),
    )(*arrays)


def shape_of(shape, dtype):
    return jax.ShapeDtypeStruct(shape, dtype)


def shift_cols(array, step):
    chips, cores = lax.axis_size("chips"), lax.axis_size("core")
    total = chips * cores
    pairs = [(i, i + step) for i in range(total) if 0 <= i + step < total]
    return lax.ppermute(array, ("chips", "core"), pairs)


def shift_rows(array, step):
    total = lax.axis_size("rows")
    pairs = [(i, i + step) for i in range(total) if 0 <= i + step < total]
    return lax.ppermute(array, "rows", pairs)


def extended(array, row_dim):
    length = array.shape[row_dim]
    before = shift_rows(lax.slice_in_dim(array, length - 1, length, axis=row_dim), 1)
    after = shift_rows(lax.slice_in_dim(array, 0, 1, axis=row_dim), -1)
    array = jnp.concatenate([before, array, after], axis=row_dim)
    dim = row_dim + 1
    length = array.shape[dim]
    before = shift_cols(lax.slice_in_dim(array, length - 1, length, axis=dim), 1)
    after = shift_cols(lax.slice_in_dim(array, 0, 1, axis=dim), -1)
    return jnp.concatenate([before, array, after], axis=dim)


def spread_all(stats):
    return lax.all_to_all(stats, EVERY, 0, 0)


def swap(array, axis, flip):
    total = lax.axis_size(axis)
    return lax.ppermute(array, axis, [(i, i ^ flip) for i in range(total)])


def spread_chips(shard):
    chips, rows = lax.axis_size("chips"), lax.axis_size("rows")
    width = shard.shape[-1] // rows
    mine = lax.dynamic_slice_in_dim(shard, lax.axis_index("rows") * width, width, axis=2)
    return [swap(mine, "chips", hop) for hop in range(1, chips)]


def spread_rows(shard, hops):
    line = jnp.stack(hops)
    return [shard, line] + [swap(line, "rows", flip) for flip in range(1, lax.axis_size("rows"))]


def spread_cores(pieces):
    return pieces + [swap(piece, "core", 1) for piece in pieces]


def gather_weights(shard):
    rows = lax.axis_size("rows")
    part = shard.shape[1] // rows
    mine = lax.dynamic_slice_in_dim(shard, lax.axis_index("rows") * part, part, axis=1)
    return lax.all_gather(mine.astype(BF16), ("chips", "core", "rows"), axis=1, tiled=True)


def pick(array, axis, index):
    return lax.dynamic_index_in_dim(array, index, axis=axis, keepdims=False)


def summed(parts):
    total = parts[0].astype(F32)
    for part in parts[1:]:
        total = total + part.astype(F32)
    return total.astype(BF16)


def reduce_rows(half):
    groups, depth, width = half.shape
    rows, chips = lax.axis_size("rows"), lax.axis_size("chips")
    row = lax.axis_index("rows")
    parts = half.reshape(groups, chips, 2, rows, depth // (2 * rows * chips), width)
    mine = pick(parts, 3, row)
    return [mine] + [swap(pick(parts, 3, row ^ flip), "rows", flip) for flip in range(1, rows)]


def reduce_chips(parts):
    total = summed(parts)
    chip = lax.axis_index("chips")
    chips = lax.axis_size("chips")
    return [pick(total, 1, chip)] + [
        swap(pick(total, 1, chip ^ hop), "chips", hop) for hop in range(1, chips)
    ]


def share_rows(parts):
    total = summed(parts)
    core = lax.axis_index("core")
    kept = pick(total, 1, core)
    got = swap(pick(total, 1, 1 - core), "core", 1)
    low = jnp.where(core == 0, kept, got)
    high = jnp.where(core == 0, got, kept)
    share = jnp.concatenate([low, high], axis=-1)
    return [share] + [swap(share, "rows", flip) for flip in range(1, lax.axis_size("rows"))]


def reduce_half(half):
    return share_rows(reduce_chips(reduce_rows(half)))


def update_kernel(rate, count, place_ref, weight_ref, moment_ref, average_ref, *refs):
    parts, outs = refs[:count], refs[-4:]
    turn = pl.program_id(1)
    for flip, part in enumerate(parts):

        @pl.when(turn == flip)
        def _():
            grad = part[...].astype(F32)[:, None]
            weight = weight_ref[...]
            descent = grad + WEIGHT_DECAY * weight
            mom_new = MOMENTUM * moment_ref[...] + descent
            weight_new = weight - rate * (descent + MOMENTUM * mom_new)
            outs[0][...] = grad
            outs[1][...] = mom_new
            outs[2][...] = weight_new
            outs[3][...] = AVERAGE * average_ref[...] + (1.0 - AVERAGE) * weight_new


def update(parts, weight, moment, average, rate, first, block, earlier=()):
    groups, depth, channels = weight.shape
    rows = lax.axis_size("rows")
    piece = depth // rows
    count = parts[0].shape[0]
    split = (groups, rows, piece, channels)
    weight, moment, average = (a.reshape(split) for a in (weight, moment, average))
    earlier = [a.reshape(split) for a in earlier]
    state = pl.BlockSpec(
        (block, 1, piece, channels), lambda g, t, p: (g + first // block, jnp.bitwise_xor(p[2], t), 0, 0)
    )
    grads = pl.BlockSpec((block, piece, channels), lambda g, t, p: (g, 0, 0))
    anywhere = pl.BlockSpec(memory_space=pl.ANY)
    outs = pl.pallas_call(
        functools.partial(update_kernel, rate, len(parts)),
        grid_spec=pltpu.PrefetchScalarGridSpec(
            num_scalar_prefetch=1,
            grid=(count // block, rows),
            in_specs=[state] * 3 + [grads] * len(parts) + [anywhere] * len(earlier),
            out_specs=[state] * 4,
        ),
        out_shape=[jax.ShapeDtypeStruct(split, F32)] * 4,
        input_output_aliases={4 + len(parts) + i: i for i in range(len(earlier))},
        compiler_params=pltpu.CompilerParams(vmem_limit_bytes=VMEM_LIMIT),
        cost_estimate=pl.CostEstimate(
            flops=0, bytes_accessed=30 * count * depth * channels, transcendentals=0
        ),
    )(place_of(), weight, moment, average, *parts, *earlier)
    return [a.reshape(groups, depth, channels) for a in outs]


def place_of():
    place = jnp.stack([lax.axis_index("chips"), lax.axis_index("core"), lax.axis_index("rows")])
    return place.astype(jnp.int32)


def halves(array):
    core = lax.axis_index("core")
    half = array.shape[-1] // 2
    mine = lax.dynamic_slice_in_dim(array, core * half, half, axis=array.ndim - 1)
    other = lax.dynamic_slice_in_dim(array, (1 - core) * half, half, axis=array.ndim - 1)
    return mine, lax.ppermute(other, "core", PAIR)


def refresh(weight, gradient, moment, average, step_rate):
    descent = gradient + WEIGHT_DECAY * weight
    mom_new = MOMENTUM * moment + descent
    weight_new = weight - step_rate * (descent + MOMENTUM * mom_new)
    avg_new = AVERAGE * average + (1.0 - AVERAGE) * weight_new
    return (mom_new, weight_new, avg_new)


def shards(
    features,
    extent,
    cotangent,
    wide_w,
    wide_mom,
    wide_avg,
    point_w,
    point_mom,
    point_avg,
    norm_w,
    norm_mom,
    norm_avg,
):
    tasks = point_w.shape[0] // 2
    images, rows, cols, channels = features.shape
    half_rows, half_cols = rows // 2, cols // 2
    rate_wide = 0.4 / (9.0 * channels) ** 0.5
    rate_point = 2.0 / float(channels) ** 0.5
    devices = lax.axis_size("rows") * lax.axis_size("chips") * lax.axis_size("core")
    row_start = lax.axis_index("rows") * rows
    col_start = (lax.axis_index("chips") * lax.axis_size("core") + lax.axis_index("core")) * cols
    starts = jnp.stack([row_start, col_start]).astype(jnp.int32)[:, None]
    full_ext = jnp.broadcast_to((extent - starts)[:, :, None], (2, images, channels))
    half_ext = jnp.broadcast_to((extent // 2 - starts // 2)[:, :, None], (2, images, channels))
    full_count = jnp.sum(extent[0] * extent[1]).astype(F32)
    meta = jnp.broadcast_to(
        jnp.stack([1.0 / full_count, 4.0 / full_count, lax.rsqrt(full_count / 16.0)])[:, None],
        (3, channels),
    )
    place = place_of()
    shared_own = wide_w[:1].astype(BF16)
    hops = spread_chips(shared_own)
    features, hops[0] = lax.optimization_barrier((features, hops[0]))
    pieces = spread_rows(shared_own, hops)
    point_full = gather_weights(point_w)
    first_w, second_w = point_full[:tasks], point_full[tasks:]

    maps = features.transpose(1, 2, 0, 3)
    row_ids = jnp.arange(rows, dtype=jnp.int32)[:, None, None]
    col_ids = jnp.arange(cols, dtype=jnp.int32)[None, :, None]
    inside = (row_ids < (extent[0] - row_start)[None, None]) & (col_ids < (extent[1] - col_start)[None, None])
    maps = jnp.where(inside[..., None], maps, jnp.zeros((), BF16))
    x_pad = extended(maps, 0)
    pieces, x_pad = lax.optimization_barrier((pieces, x_pad))
    later_w, _ = lax.optimization_barrier((wide_w[1:], pieces))
    branch_w = gather_weights(later_w)
    branch_in = (branch_w, leading((1,) + branch_w.shape[1:]))
    pieces = spread_cores(pieces)
    x_other = lax.ppermute(x_pad, "core", PAIR)
    cot = cotangent.transpose(0, 2, 3, 1, 4)

    full = (rows, cols, images, channels)
    half = (half_rows, half_cols, images, channels)
    wide = (half_rows + 2, half_cols + 2, images, channels)
    quarter = (half_rows // 2, half_cols // 2, images, channels)
    stat = (devices, 2, channels)
    task_stat = (devices, tasks, 2, channels)
    one_stat = second_dim((devices, 1, 2, channels))
    meta_in = (meta, whole(meta.shape))
    norm_in = (norm_w, whole(norm_w.shape))
    full_in = (full_ext, whole(full_ext.shape))
    half_in = (half_ext, whole(half_ext.shape))
    vec = pltpu.VMEM((2, channels), F32)
    place_in = (place, pl.BlockSpec(memory_space=pltpu.SMEM))
    anywhere = pl.BlockSpec(memory_space=pl.ANY)
    copies = 2 * (1 + lax.axis_size("rows") * (lax.axis_size("chips") - 1))

    def weight_room(slots):
        shape = (slots, 9 * channels, channels) if slots > 1 else (9 * channels, channels)
        return [pltpu.VMEM(shape, BF16), pltpu.SemaphoreType.DMA((slots, copies))]

    full_flops = 2 * 9 * rows * cols * images * channels * channels
    half_flops = full_flops // 4 * tasks
    task_of = lambda shape: leading((1,) + shape)

    block = 4
    z, local = call(
        functools.partial(shared_fwd_kernel, block),
        rows // block,
        [place_in, (x_pad, whole(x_pad.shape)), full_in] + [(p, anywhere) for p in pieces],
        [(shape_of(full, F32), leading((block,) + full[1:])), (shape_of(stat, F32), whole(stat))],
        [vec] + weight_room(1),
        full_flops,
    )
    stat0 = spread_all(local)

    pooled, local = call(
        functools.partial(pool_kernel, block),
        rows // block,
        [
            (z, leading((block,) + full[1:])),
            (stat0, whole(stat)),
            meta_in,
            norm_in,
            full_in,
            (first_w, whole(first_w.shape)),
        ],
        [
            (shape_of(half, BF16), leading((block // 2,) + half[1:])),
            (shape_of(task_stat, F32), whole(task_stat)),
        ],
        [pltpu.VMEM(half, BF16), vec],
    )
    pooled_wide = extended(pooled, 0)
    stat1 = spread_all(local)

    first, hidden, second, local = call(
        attend_kernel,
        tasks,
        [
            (pooled_wide, whole(wide)),
            (stat1, one_stat),
            meta_in,
            norm_in,
            half_in,
            (first_w, task_of(first_w.shape[1:])),
            (second_w, task_of(second_w.shape[1:])),
        ],
        [
            (shape_of((tasks,) + half, F32), task_of(half)),
            (shape_of((tasks,) + half, BF16), task_of(half)),
            (shape_of((tasks,) + wide, F32), task_of(wide)),
            (shape_of(task_stat, F32), one_stat),
        ],
    )
    stat2 = spread_all(local)

    masked, branch, local = call(
        branch_fwd_kernel,
        tasks,
        [
            (second, task_of(wide)),
            (pooled_wide, whole(wide)),
            (stat2, one_stat),
            meta_in,
            norm_in,
            half_in,
            branch_in,
        ],
        [
            (shape_of((tasks,) + wide, BF16), task_of(wide)),
            (shape_of((tasks,) + half, F32), task_of(half)),
            (shape_of(task_stat, F32), one_stat),
        ],
        flops=half_flops,
    )
    masked_other = lax.ppermute(masked, "core", PAIR)
    stat3 = spread_all(local)

    branch_ins = [
        (branch, task_of(half)),
        (cot, task_of(quarter)),
        (stat3, one_stat),
    ]
    result, local = call(
        result_kernel,
        tasks,
        branch_ins + [meta_in, norm_in, half_in],
        [
            (shape_of((tasks,) + quarter, BF16), task_of(quarter)),
            (shape_of(task_stat, F32), one_stat),
        ],
    )
    back3 = spread_all(local)

    (branch_dz,) = call(
        branch_dz_kernel,
        tasks,
        branch_ins + [(back3, one_stat), meta_in, norm_in, half_in],
        [(shape_of((tasks,) + half, BF16), task_of(half))],
    )
    dz_own, dz_other = halves(branch_dz)
    dz_wide = extended(branch_dz, 1)
    narrow = half[:-1] + (channels // 2,)
    (branch_grad,) = call(
        branch_wgrad_kernel,
        tasks,
        [
            (masked, task_of(wide)),
            (masked_other, task_of(wide)),
            (dz_own, task_of(narrow)),
            (dz_other, task_of(narrow)),
        ],
        [
            (
                shape_of((tasks, 9, channels, channels // 2), BF16),
                task_of((9, channels, channels // 2)),
            )
        ],
        flops=half_flops,
    )
    branch_share = reduce_half(branch_grad.reshape(tasks, 9 * channels, channels // 2))

    ga, product, local = call(
        branch_dgrad_kernel,
        tasks,
        [
            (dz_wide, task_of(wide)),
            branch_in,
            (second, task_of(wide)),
            (pooled, whole(half)),
            (stat2, one_stat),
            meta_in,
            norm_in,
        ],
        [
            (shape_of((tasks,) + half, F32), task_of(half)),
            (shape_of(half, F32), whole(half)),
            (shape_of(task_stat, F32), one_stat),
        ],
        flops=half_flops,
    )
    back2 = spread_all(local)

    square = (channels, channels)
    second_grad, gl, local = call(
        attend_back_kernel,
        tasks,
        [
            (ga, task_of(half)),
            (second, task_of(wide)),
            (stat2, one_stat),
            (back2, one_stat),
            (hidden, task_of(half)),
            (second_w, task_of(square)),
            (first, task_of(half)),
            (stat1, one_stat),
            meta_in,
            norm_in,
            half_in,
        ],
        [
            (shape_of((tasks,) + square, BF16), task_of(square)),
            (shape_of((tasks,) + half, F32), task_of(half)),
            (shape_of(task_stat, F32), one_stat),
        ],
    )
    back1 = spread_all(local)

    first_grad, grad_pooled, local = call(
        functools.partial(pooled_back_kernel, block),
        tasks,
        [
            (gl, task_of(half)),
            (first, task_of(half)),
            (stat1, one_stat),
            (back1, one_stat),
            (pooled, whole(half)),
            (first_w, task_of(square)),
            (product, whole(half)),
            (z, whole(full)),
            (stat0, whole(stat)),
            meta_in,
            norm_in,
            half_in,
            full_in,
        ],
        [
            (shape_of((tasks,) + square, BF16), task_of(square)),
            (shape_of(half, F32), whole(half)),
            (shape_of(stat, F32), whole(stat)),
        ],
    )
    back0 = spread_all(local)
    point_local = jnp.concatenate([first_grad, second_grad], axis=0)
    point_own, point_other = halves(point_local)
    point_share = reduce_half(point_own + point_other)

    (shared_dz,) = call(
        functools.partial(shared_dz_kernel, block),
        rows // block,
        [
            (z, leading((block,) + full[1:])),
            (grad_pooled, leading((block // 2,) + half[1:])),
            (stat0, whole(stat)),
            (back0, whole(stat)),
            meta_in,
            norm_in,
            full_in,
        ],
        [(shape_of(full, BF16), leading((block,) + full[1:]))],
    )
    dz_own, dz_other = halves(shared_dz)
    (shared_grad,) = call(
        shared_wgrad_kernel,
        9,
        [
            (x_pad, whole(x_pad.shape)),
            (x_other, whole(x_other.shape)),
            (dz_own, whole(dz_own.shape)),
            (dz_other, whole(dz_other.shape)),
        ],
        [(shape_of((9, channels, channels // 2), BF16), leading((1, channels, channels // 2)))],
        flops=full_flops,
    )
    shared_share = reduce_half(shared_grad.reshape(1, 9 * channels, channels // 2))
    dz_pad = extended(shared_dz, 0)
    (input_grad,) = call(
        functools.partial(shared_dgrad_kernel, block),
        rows // block,
        [place_in, (dz_pad, whole(dz_pad.shape)), full_in] + [(p, anywhere) for p in pieces],
        [(shape_of(full, F32), leading((block,) + full[1:]))],
        weight_room(1),
        full_flops,
    )
    input_grad = input_grad.transpose(2, 0, 1, 3)

    branch_state = update(branch_share, wide_w, wide_mom, wide_avg, rate_wide, 1, 1)
    wide_share, wide_mom_new, wide_new, wide_avg_new = update(
        shared_share, wide_w, wide_mom, wide_avg, rate_wide, 0, 1, branch_state
    )
    point_share, point_mom_new, point_new, point_avg_new = update(
        point_share, point_w, point_mom, point_avg, rate_point, 0, 2 * tasks
    )
    bsum = jnp.stack([jnp.sum(b, axis=0) for b in (back1, back2, back3)], axis=1)
    bsum = bsum.transpose(2, 0, 1, 3).reshape(2, 3 * tasks, channels)
    norm_grad = jnp.concatenate([jnp.sum(back0, axis=0)[:, None], bsum], axis=1)[::-1]
    norm_mom_new, norm_new, norm_avg_new = refresh(norm_w, norm_grad, norm_mom, norm_avg, RATE_NORM)
    return (
        result.transpose(0, 3, 1, 2, 4),
        input_grad,
        wide_share,
        wide_mom_new,
        wide_new,
        wide_avg_new,
        point_share,
        point_mom_new,
        point_new,
        point_avg_new,
        norm_grad,
        norm_mom_new,
        norm_new,
        norm_avg_new,
    )


def solution(mesh):
    rows, cols = mesh.devices.shape
    cores = 2
    fine = Mesh(mesh.devices.reshape(rows, cols // cores, cores), EVERY)
    across = ("chips", "core")
    weights = P(None, across, None)
    placed = (
        P(None, "rows", across, None),
        P(),
        P(None, None, "rows", across, None),
        weights,
        weights,
        weights,
        weights,
        weights,
        weights,
        P(),
        P(),
        P(),
    )
    return jax.shard_map(
        shards,
        mesh=fine,
        in_specs=placed,
        out_specs=(
            P(None, None, "rows", across, None),
            P(None, "rows", across, None),
            weights,
            weights,
            weights,
            weights,
            weights,
            weights,
            weights,
            weights,
            P(),
            P(),
            P(),
            P(),
        ),
        check_vma=False,
    )
```

time: 930 us -> 667 us (0.72)
  blocking collectives: 343 us -> 61.9 us
  Pallas kernels: 0 us -> 156 us
  matrix products: 131 us -> 0 us
  starting transfers between devices: 38.6 us -> 133 us
  waiting for transfers between devices: 263 us -> 215 us
  other arithmetic: 70.8 us -> 27.8 us
  local copies, waits for them, and re-layouts: 61.9 us -> 50.3 us
    psum x8 -> x0, blocking collectives: 343 us -> none  [the longest x4 178 us: norm_forward(): summed, squares = lax.psum((summed, squares), ('rows', 'cols'))]
    reduce_scatter x2 -> x0, waiting for transfers between devices: 163 us -> none  [the longest x1 163 us: shards(): lax.psum_scatter(wide_local.astype(jnp.bfloat16), 'cols', scatter_dimensi...]
    pallas_call x0 -> x16, Pallas kernels: none -> 156 us  [the longest x13 130 us: call(): pl.pallas_call(kernel, grid=(grid,), in_specs=[spec for _, spec in ins],...]
    dot_general x60 -> x0, matrix products: 131 us -> none  [the longest x18 59.5 us: taps_input(): jnp.einsum(pattern, flipped(padded, offset, tile_rows, tile_cols), weight...]
    ppermute x16 -> x62, waiting for transfers between devices: 8.61 us -> 115 us  [the longest x41 108 us: swap(): return lax.ppermute(array, axis, [(i, i ^ flip) for i in range(total)])]
    all_to_all x0 -> x5, waiting for transfers between devices: none -> 82.8 us  [spread_all(): return lax.all_to_all(stats, EVERY, 0, 0)]
    ppermute x16 -> x62, starting transfers between devices: 38.4 us -> 102 us  [the longest x41 50.6 us: swap(): return lax.ppermute(array, axis, [(i, i ^ flip) for i in range(total)])]
    all_to_all x0 -> x3, blocking collectives: none -> 61.9 us  [spread_all(): return lax.all_to_all(stats, EVERY, 0, 0)]
  transfers between devices with their start and end apart: 22 -> 69, of which waited for: 7 -> 34; matrix products, arithmetic and copies ran while one was open for 18% -> 10% of each run, Pallas kernels for 0% -> 20%
where the time goes in v1:
time: 667 us; the launch traced here: 661 us
  waiting for transfers between devices  215 us (32%)
  Pallas kernels  156 us (23%)
  starting transfers between devices  133 us (20%)
  blocking collectives  61.9 us (9%)
  local copies, waits for them, and re-layouts  50.3 us (8%)
  other arithmetic  27.8 us (4%)
  between operations  16 us (2%)
    pallas_call x13, Pallas kernels, call(): pl.pallas_call(kernel, grid=(grid,), in_specs=[spec for _, spec in ins],...  130 us
    ppermute x41, waiting for transfers between devices, swap(): return lax.ppermute(array, axis, [(i, i ^ flip) for i in range(total)])  108 us
    all_to_all x5, waiting for transfers between devices, spread_all(): return lax.all_to_all(stats, EVERY, 0, 0)  82.8 us
    all_to_all x3, blocking collectives, spread_all(): return lax.all_to_all(stats, EVERY, 0, 0)  61.9 us
    ppermute x41, starting transfers between devices, swap(): return lax.ppermute(array, axis, [(i, i ^ flip) for i in range(total)])  50.6 us
    ppermute x8, starting transfers between devices, shift_rows(): return lax.ppermute(array, 'rows', pairs)  32.2 us
    all_to_all x5, starting transfers between devices, spread_all(): return lax.all_to_all(stats, EVERY, 0, 0)  31.7 us
    pallas_call x3, Pallas kernels, update(): pl.pallas_call(functools.partial(update_kernel, rate, len(parts)), grid_s...  25.7 us
  transfers between devices with their start and end apart: 69, of which 34 were waited for; matrix products, arithmetic and copies ran while one was open for 10% of the time, Pallas kernels for 20%

profile of v1, /device:TPU:0, one launch (start us, length us, event | category | flops | bytes accessed | tf_op | source)
XLA Modules:
  0.0 660.5 jit_solution(3081085900125018831)
XLA Ops:
  36.0 9.2 %collective-permute-done.2 = bf16[1,576,128]{2,1,0:T(8,128)(2,1)S(1)} collective-permute-done((bf16[1,576,128]{2,1,0:T(8,128)(2,1)S(1)}, bf16[1,576,128]{2,1,0:T(8,128)(2,1)S(1)}, u32[]{:S(2)}, u32[]{:S(2)}) %collective-permute-start.2) | collective-permute-done | bytes 147488 | tf_op jit(solution)/shard_map/ppermute | solution.py:458
  45.3 9.4 %collective-permute-done.1 = bf16[1,576,128]{2,1,0:T(8,128)(2,1)S(1)} collective-permute-done((bf16[1,576,128]{2,1,0:T(8,128)(2,1)S(1)}, bf16[1,576,128]{2,1,0:T(8,128)(2,1)S(1)}, u32[]{:S(2)}, u32[]{:S(2)}) %collective-permute-start.1) | collective-permute-done | bytes 147488 | tf_op jit(solution)/shard_map/ppermute | solution.py:458
  74.0 8.6 %collective-permute-done.4.refs_3_ = bf16[3,1,576,128]{3,2,1,0:T(8,128)(2,1)} collective-permute-done((bf16[3,1,576,128]{3,2,1,0:T(8,128)(2,1)}, bf16[3,1,576,128]{3,2,1,0:T(8,128)(2,1)}, u32[]{:S(2)}, u32[]{:S(2)}) %collective-permute-start.4) | collective-permute-done | bytes 442400 | tf_op jit(solution)/shard_map/ppermute | solution.py:458
  92.5 14.0 %shard_map.227 = (f32[24,4,16,512]{3,2,1,0:T(8,128)}, f32[32,2,512]{2,1,0:T(2,128)}) custom-call(s32[3]{0:T(128)} %pad_add_fusion.place_ref, bf16[26,6,16,512]{3,2,1,0:T(8,128)(2,1)} %pad_maximum_fusion.1.x_ref.own_ref, s32[2,16,512]{2,1,0:T(8,128)} %broadcast_in_dim.18.ext_ref.full_ref, bf16[1,576,512]{2,1,0:T(8,128)(2,1)} %copy-done.15, ...), custom_call_target="tpu_custom_call" | custom-call | flops 7247757312 | bytes 10616844 | tf_op jit(solution)/shard_map/pallas_call | solution.py:411
  146.3 13.8 %all-to-all-done.1.stat_ref.stat1_ref = f32[32,3,2,512]{3,2,1,0:T(2,128)S(1)} async-done(((f32[32,3,2,512]{3,2,1,0:T(2,128)}), f32[32,3,2,512]{3,2,1,0:T(2,128)S(1)}, u32[]{:S(2)}, u32[]{:S(2)}) %all-to-all-start.1) | async-done | bytes 393248 | tf_op jit(solution)/shard_map/all_to_all | solution.py:453
  160.9 8.3 %shard_map.229 = (f32[3,12,2,16,512]{4,3,2,1,0:T(8,128)}, bf16[3,12,2,16,512]{4,3,2,1,0:T(8,128)(2,1)}, f32[3,14,4,16,512]{4,3,2,1,0:T(8,128)}, f32[32,3,2,512]{3,2,1,0:T(2,128)}) custom-call(bf16[14,4,16,512]{3,2,1,0:T(8,128)(2,1)} %pad_maximum_fusion.4.pe_ref, f32[32,3,2,512]{3,2,1,0:T(2,128)} %copy-done.4, f32[3,512]{1,0:T(4,128)} %broadcast_in_dim.19.meta_ref, ...), custom_call_target="tpu_custom_call" | custom-call | bytes 14006272 | tf_op jit(solution)/shard_map/pallas_call | solution.py:411
  169.2 27.7 %all_to_all.40.stat_ref.stat2_ref = f32[32,3,2,512]{3,2,1,0:T(2,128)} all-to-all(f32[32,3,2,512]{3,2,1,0:T(2,128)} %get-tuple-element.70), channel_id=1, replica_groups=mesh['rows'=4,'chips'=4,'core'=2] {'rows','chips','core'}, dimensions={0} | all-to-all | bytes 786432 | tf_op jit(solution)/shard_map/all_to_all | solution.py:453
  196.9 17.4 %all-gather.5.cloned.1.call-done.w_ref = bf16[3,4608,512]{2,1,0:T(8,128)(2,1)} async-done(((bf16[3,144,512]{2,1,0:T(8,128)(2,1)}), bf16[3,4608,512]{2,1,0:T(8,128)(2,1)}) %all-gather.5.cloned.1.call-update) | async-done | bytes 14155792 | tf_op jit(solution)/shard_map/all_gather | solution.py:481
  214.3 12.5 %shard_map.230 = (bf16[3,14,4,16,512]{4,3,2,1,0:T(8,128)(2,1)}, f32[3,12,2,16,512]{4,3,2,1,0:T(8,128)}, f32[32,3,2,512]{3,2,1,0:T(2,128)}) custom-call(f32[3,14,4,16,512]{4,3,2,1,0:T(8,128)} %get-tuple-element.69.second_ref, bf16[14,4,16,512]{3,2,1,0:T(8,128)(2,1)} %pad_maximum_fusion.4.pe_ref, f32[32,3,2,512]{3,2,1,0:T(2,128)} %all_to_all.40.stat_ref.stat2_ref, ...), custom_call_target="tpu_custom_call" | custom-call | flops 5435817984 | bytes 26589184 | tf_op jit(solution)/shard_map/pallas_call | solution.py:411
  226.8 17.3 %all_to_all.41.stat_ref = f32[32,3,2,512]{3,2,1,0:T(2,128)} all-to-all(f32[32,3,2,512]{3,2,1,0:T(2,128)} %get-tuple-element.73), channel_id=1, replica_groups=mesh['rows'=4,'chips'=4,'core'=2] {'rows','chips','core'}, dimensions={0} | all-to-all | bytes 786432 | tf_op jit(solution)/shard_map/all_to_all | solution.py:453
  248.6 16.8 %all_to_all.42.back_ref = f32[32,3,2,512]{3,2,1,0:T(2,128)} all-to-all(f32[32,3,2,512]{3,2,1,0:T(2,128)} %get-tuple-element.75), channel_id=1, replica_groups=mesh['rows'=4,'chips'=4,'core'=2] {'rows','chips','core'}, dimensions={0} | all-to-all | bytes 786432 | tf_op jit(solution)/shard_map/all_to_all | solution.py:453
  288.9 14.0 %shard_map.233 = (f32[3,12,2,16,512]{4,3,2,1,0:T(8,128)}, f32[12,2,16,512]{3,2,1,0:T(8,128)}, f32[32,3,2,512]{3,2,1,0:T(2,128)}) custom-call(bf16[3,14,4,16,512]{4,3,2,1,0:T(8,128)(2,1)} %pad_maximum_fusion.dz_ref, bf16[3,4608,512]{2,1,0:T(8,128)(2,1)} %all-gather.5.cloned.1.call-done.w_ref, f32[3,14,4,16,512]{4,3,2,1,0:T(8,128)} %get-tuple-element.69.second_ref, ...), custom_call_target="tpu_custom_call" | custom-call | flops 5435817984 | bytes 26785792 | tf_op jit(solution)/shard_map/pallas_call | solution.py:411
  302.9 13.0 %all-to-all-start.5 = ((f32[32,3,2,512]{3,2,1,0:T(2,128)}), f32[32,3,2,512]{3,2,1,0:T(2,128)S(1)}, u32[]{:S(2)}, u32[]{:S(2)}) async-start(f32[32,3,2,512]{3,2,1,0:T(2,128)} %get-tuple-element.77), calls=%async_computation.5 | async-start | bytes 786432 | tf_op jit(solution)/shard_map/all_to_all | solution.py:453
  317.4 12.1 %all-to-all-done.5.back_ref = f32[32,3,2,512]{3,2,1,0:T(2,128)S(1)} async-done(((f32[32,3,2,512]{3,2,1,0:T(2,128)}), f32[32,3,2,512]{3,2,1,0:T(2,128)S(1)}, u32[]{:S(2)}, u32[]{:S(2)}) %all-to-all-start.5) | async-done | bytes 393248 | tf_op jit(solution)/shard_map/all_to_all | solution.py:453
  330.2 9.6 %shard_map.234 = (bf16[3,512,512]{2,1,0:T(8,128)(2,1)}, f32[3,12,2,16,512]{4,3,2,1,0:T(8,128)}, f32[32,3,2,512]{3,2,1,0:T(2,128)}) custom-call(f32[3,12,2,16,512]{4,3,2,1,0:T(8,128)} %get-tuple-element.76.ga_ref, f32[3,14,4,16,512]{4,3,2,1,0:T(8,128)} %get-tuple-element.69.second_ref, f32[32,3,2,512]{3,2,1,0:T(2,128)} %all_to_all.40.stat_ref.stat2_ref, ...), custom_call_target="tpu_custom_call" | custom-call | bytes 18593792 | tf_op jit(solution)/shard_map/pallas_call | solution.py:411
  343.3 11.0 %shard_map.239 = bf16[3,9,512,256]{3,2,1,0:T(8,128)(2,1)} custom-call(bf16[3,14,4,16,512]{4,3,2,1,0:T(8,128)(2,1)} %get-tuple-element.85.own_ref, bf16[3,14,4,16,512]{4,3,2,1,0:T(8,128)(2,1)} %collective-permute-done.39.other_ref, bf16[3,12,2,16,256]{4,3,2,1,0:T(8,128)(2,1)} %get-tuple-element.148.dz_own_ref, bf16[3,12,2,16,256]{4,3,2,1,0:T(8,128)(2,1)} %copy-done.38), custom_call_target="tpu_custom_call" | custom-call | flops 5435817984 | bytes 13762560 | tf_op jit(solution)/shard_map/pallas_call | solution.py:411
  366.6 11.6 %shard_map.235 = (bf16[3,512,512]{2,1,0:T(8,128)(2,1)}, f32[12,2,16,512]{3,2,1,0:T(8,128)}, f32[32,2,512]{2,1,0:T(2,128)}) custom-call(f32[3,12,2,16,512]{4,3,2,1,0:T(8,128)} %get-tuple-element.80.gl_ref, f32[3,12,2,16,512]{4,3,2,1,0:T(8,128)} %get-tuple-element.79.first_ref, f32[32,3,2,512]{3,2,1,0:T(2,128)} %copy-done.4, f32[32,3,2,512]{3,2,1,0:T(2,128)} %copy-done.7, ...), custom_call_target="tpu_custom_call" | custom-call | bytes 14202880 | tf_op jit(solution)/shard_map/pallas_call | solution.py:411
  389.8 50.8 %all-to-all-done.7.back_ref = f32[32,2,512]{2,1,0:T(2,128)S(1)} async-done(((f32[32,2,512]{2,1,0:T(2,128)}), f32[32,2,512]{2,1,0:T(2,128)S(1)}, u32[]{:S(2)}, u32[]{:S(2)}) %all-to-all-start.7) | async-done | bytes 131104 | tf_op jit(solution)/shard_map/all_to_all | solution.py:453
  449.4 12.2 %collective-permute-start.24 = (bf16[1,4,16,512]{3,2,1,0:T(8,128)(2,1)}, bf16[1,4,16,512]{3,2,1,0:T(8,128)(2,1)S(1)}, u32[]{:S(2)}, u32[]{:S(2)}) collective-permute-start(bf16[1,4,16,512]{3,2,1,0:T(8,128)(2,1)} %get-tuple-element.142), channel_id=1, source_target_pairs={{8,0},{16,8},{24,16},{9,1},{17,9},{25,17},{10,2},{18,10},{26,18},{... | collective-permute-start | bytes 196616 | tf_op jit(solution)/shard_map/ppermute | solution.py:437
  486.5 13.2 %shard_map.238 = bf16[9,512,256]{2,1,0:T(8,128)(2,1)} custom-call(bf16[26,6,16,512]{3,2,1,0:T(8,128)(2,1)} %pad_maximum_fusion.1.x_ref.own_ref, bf16[26,6,16,512]{3,2,1,0:T(8,128)(2,1)} %collective-permute-done.27.other_ref, bf16[24,4,16,256]{3,2,1,0:T(8,128)(2,1)} %get-tuple-element.140.dz_own_ref, bf16[24,4,16,256]{3,2,1,0:T(8,128)(2,1)} %copy-done.36), custom_call_target="tpu_custom_call" | custom-call | flops 7247757312 | bytes 9043968 | tf_op jit(solution)/shard_map/pallas_call | solution.py:411
  503.8 20.0 %collective-permute-done.45 = bf16[3,2,144,256]{3,2,0,1:T(8,128)(2,1)S(1)} collective-permute-done((bf16[3,2,144,256]{3,2,0,1:T(8,128)(2,1)}, bf16[3,2,144,256]{3,2,0,1:T(8,128)(2,1)S(1)}, u32[]{:S(2)}, u32[]{:S(2)}) %collective-permute-start.45) | collective-permute-done | bytes 442400 | tf_op jit(solution)/shard_map/ppermute | solution.py:458
  541.7 12.2 %collective-permute-done.30 = bf16[1,4,2,144,256]{4,3,2,1,0:T(8,128)(2,1)S(1)} collective-permute-done((bf16[1,4,2,144,256]{4,3,2,1,0:T(8,128)(2,1)S(1)}, bf16[1,4,2,144,256]{4,3,2,1,0:T(8,128)(2,1)S(1)}, u32[]{:S(2)}, u32[]{:S(2)}) %collective-permute-start.30) | collective-permute-done | bytes 589856 | tf_op jit(solution)/shard_map/ppermute | solution.py:458
  607.0 13.7 %shard_map.237 = f32[24,4,16,512]{3,2,1,0:T(8,128)} custom-call(s32[3]{0:T(128)} %pad_add_fusion.place_ref, bf16[26,6,16,512]{3,2,1,0:T(8,128)(2,1)} %pad_maximum_fusion.2.dz_ref, s32[2,16,512]{2,1,0:T(8,128)} %broadcast_in_dim.18.ext_ref.full_ref, bf16[1,576,512]{2,1,0:T(8,128)(2,1)} %copy-done.15, bf16[3,1,576,128]{3,2,1,0:T(8,128)(2,1)} %pad_maximum_fusion.5.refs_1_, ...), custom_call_target="tpu_custom_call" | custom-call | flops 7247757312 | bytes 10485772 | tf_op jit(solution)/shard_map/pallas_call | solution.py:411
  626.4 14.7 %shard_map.240 = (f32[4,4,144,512]{3,2,1,0:T(8,128)}, f32[4,4,144,512]{3,2,1,0:T(8,128)}, f32[4,4,144,512]{3,2,1,0:T(8,128)}, f32[4,4,144,512]{3,2,1,0:T(8,128)}) custom-call(s32[3]{0:T(128)} %pad_add_fusion.place_ref, f32[4,4,144,512]{3,2,1,0:T(8,128)} %bitcast.125, f32[4,4,144,512]{3,2,1,0:T(8,128)} %bitcast.127, f32[4,4,144,512]{3,2,1,0:T(8,128)} %bitcast.129, ...), custom_call_target="tpu_custom_call" | custom-call | bytes 26542080 | tf_op jit(solution)/shard_map/pallas_call | solution.py:559
  (299 shorter events, 281.1 us)
Async XLA Ops:
  7.2 104.9 %all-gather.3.cloned.1.call-start = ((), (), s32[]{:S(2)}) async-start(), calls=%async_computation.8 | async-start | bytes 3244032 | tf_op jit(solution)/shard_map/all_gather | solution.py:481
  9.0 205.4 %all-gather.5.cloned.1.call-start = ((), (), s32[]{:S(2)}) async-start(), calls=%async_computation.9 | async-start | bytes 14598144 | tf_op jit(solution)/shard_map/all_gather | solution.py:481
  27.1 36.7 %collective-permute-start.9 = (bf16[26,1,16,512]{3,2,1,0:T(8,128)(2,1)}, bf16[26,1,16,512]{3,2,1,0:T(8,128)(2,1)}, u32[]{:S(2)}, u32[]{:S(2)}) collective-permute-start(bf16[26,1,16,512]{3,2,1,0:T(8,128)(2,1)} %get-tuple-element.134), channel_id=1, source_target_pairs={{1,0},{2,1},{3,2},{4,3},{5,4},{6,5},{7,6},{9,8},{10,9},{11,10},{12... | collective-permute-start | bytes 1277960 | tf_op jit(solution)/shard_map/ppermute | solution.py:431
  28.4 35.4 %collective-permute-start.8 = (bf16[26,1,16,512]{3,2,1,0:T(8,128)(2,1)}, bf16[26,1,16,512]{3,2,1,0:T(8,128)(2,1)}, u32[]{:S(2)}, u32[]{:S(2)}) collective-permute-start(bf16[26,1,16,512]{3,2,1,0:T(8,128)(2,1)} %get-tuple-element.133), channel_id=1, source_target_pairs={{0,1},{1,2},{2,3},{3,4},{4,5},{5,6},{6,7},{8,9},{9,10},{10,11},{11... | collective-permute-start | bytes 1277960 | tf_op jit(solution)/shard_map/ppermute | solution.py:431
  134.0 26.1 %all-to-all-start.1 = ((f32[32,3,2,512]{3,2,1,0:T(2,128)}), f32[32,3,2,512]{3,2,1,0:T(2,128)S(1)}, u32[]{:S(2)}, u32[]{:S(2)}) async-start(f32[32,3,2,512]{3,2,1,0:T(2,128)} %get-tuple-element.68), calls=%async_computation.1 | async-start | bytes 786432 | tf_op jit(solution)/shard_map/all_to_all | solution.py:453
  277.3 65.2 %collective-permute-start.39 = (bf16[3,14,4,16,512]{4,3,2,1,0:T(8,128)(2,1)}, bf16[3,14,4,16,512]{4,3,2,1,0:T(8,128)(2,1)}, u32[]{:S(2)}, u32[]{:S(2)}) collective-permute-start(bf16[3,14,4,16,512]{4,3,2,1,0:T(8,128)(2,1)} %get-tuple-element.85.own_ref), channel_id=1, source_target_pairs={{0,1},{1,0},{2,3},{3,2},{4,5},{5,4},{6,7},{7,6},{8,9},{9,8},{10,11... | collective-permute-start | bytes 8257544 | tf_op jit(solution)/shard_map/ppermute | solution.py:745
  302.9 26.6 %all-to-all-start.5 = ((f32[32,3,2,512]{3,2,1,0:T(2,128)}), f32[32,3,2,512]{3,2,1,0:T(2,128)S(1)}, u32[]{:S(2)}, u32[]{:S(2)}) async-start(f32[32,3,2,512]{3,2,1,0:T(2,128)} %get-tuple-element.77), calls=%async_computation.5 | async-start | bytes 786432 | tf_op jit(solution)/shard_map/all_to_all | solution.py:453
  317.1 167.9 %collective-permute-start.27 = (bf16[26,6,16,512]{3,2,1,0:T(8,128)(2,1)}, bf16[26,6,16,512]{3,2,1,0:T(8,128)(2,1)}, u32[]{:S(2)}, u32[]{:S(2)}) collective-permute-start(bf16[26,6,16,512]{3,2,1,0:T(8,128)(2,1)} %pad_maximum_fusion.1.x_ref.own_ref), channel_id=1, source_target_pairs={{0,1},{1,0},{2,3},{3,2},{4,5},{5,4},{6,7},{7,6},{8,9},{9,8},{10,11... | collective-permute-start | bytes 7667720 | tf_op jit(solution)/shard_map/ppermute | solution.py:647
  339.9 26.0 %all-to-all-start.6 = ((f32[32,3,2,512]{3,2,1,0:T(2,128)}), f32[32,3,2,512]{3,2,1,0:T(2,128)S(1)}, u32[]{:S(2)}, u32[]{:S(2)}) async-start(f32[32,3,2,512]{3,2,1,0:T(2,128)} %get-tuple-element.81), calls=%async_computation.6 | async-start | bytes 786432 | tf_op jit(solution)/shard_map/all_to_all | solution.py:453
  359.3 115.2 %collective-permute-start.43 = (bf16[3,4,2,144,256]{4,3,0,2,1:T(8,128)(2,1)}, bf16[3,4,2,144,256]{4,3,0,2,1:T(8,128)(2,1)}, u32[]{:S(2)}, u32[]{:S(2)}) collective-permute-start(bf16[3,4,2,144,256]{4,3,0,2,1:T(8,128)(2,1)} %bitcast.119), channel_id=1, source_target_pairs={{0,24},{8,16},{16,8},{24,0},{1,25},{9,17},{17,9},{25,1},{2,26},{10... | collective-permute-start | bytes 5308424 | tf_op jit(solution)/shard_map/ppermute | solution.py:458
  363.3 111.7 %collective-permute-start.42 = (bf16[3,4,2,144,256]{4,3,0,2,1:T(8,128)(2,1)}, bf16[3,4,2,144,256]{4,3,0,2,1:T(8,128)(2,1)}, u32[]{:S(2)}, u32[]{:S(2)}) collective-permute-start(bf16[3,4,2,144,256]{4,3,0,2,1:T(8,128)(2,1)} %bitcast.120), channel_id=1, source_target_pairs={{0,16},{8,24},{16,0},{24,8},{1,17},{9,25},{17,1},{25,9},{2,18},{10... | collective-permute-start | bytes 5308424 | tf_op jit(solution)/shard_map/ppermute | solution.py:458
  365.2 111.1 %collective-permute-start.41 = (bf16[3,4,2,144,256]{4,3,0,2,1:T(8,128)(2,1)}, bf16[3,4,2,144,256]{4,3,0,2,1:T(8,128)(2,1)}, u32[]{:S(2)}, u32[]{:S(2)}) collective-permute-start(bf16[3,4,2,144,256]{4,3,0,2,1:T(8,128)(2,1)} %bitcast.121), channel_id=1, source_target_pairs={{0,8},{8,0},{16,24},{24,16},{1,9},{9,1},{17,25},{25,17},{2,10},{10... | collective-permute-start | bytes 5308424 | tf_op jit(solution)/shard_map/ppermute | solution.py:458
  378.3 62.3 %all-to-all-start.7 = ((f32[32,2,512]{2,1,0:T(2,128)}), f32[32,2,512]{2,1,0:T(2,128)S(1)}, u32[]{:S(2)}, u32[]{:S(2)}) async-start(f32[32,2,512]{2,1,0:T(2,128)} %get-tuple-element.84), calls=%async_computation.7 | async-start | bytes 262144 | tf_op jit(solution)/shard_map/all_to_all | solution.py:453
  474.5 59.8 %collective-permute-start.51 = (bf16[6,512,256]{2,1,0:T(8,128)(2,1)}, bf16[6,512,256]{2,1,0:T(8,128)(2,1)S(1)}, u32[]{:S(2)}, u32[]{:S(2)}) collective-permute-start(bf16[6,512,256]{2,1,0:T(8,128)(2,1)} %constant_dynamic-slice_fusion.4), channel_id=1, source_target_pairs={{0,1},{1,0},{2,3},{3,2},{4,5},{5,4},{6,7},{7,6},{8,9},{9,8},{10,11... | collective-permute-start | bytes 4718600 | tf_op jit(solution)/shard_map/ppermute | solution.py:587
  475.0 55.6 %collective-permute-start.26 = (bf16[26,1,16,512]{3,2,1,0:T(8,128)(2,1)}, bf16[26,1,16,512]{3,2,1,0:T(8,128)(2,1)}, u32[]{:S(2)}, u32[]{:S(2)}) collective-permute-start(bf16[26,1,16,512]{3,2,1,0:T(8,128)(2,1)} %get-tuple-element.132), channel_id=1, source_target_pairs={{1,0},{2,1},{3,2},{4,3},{5,4},{6,5},{7,6},{9,8},{10,9},{11,10},{12... | collective-permute-start | bytes 1277960 | tf_op jit(solution)/shard_map/ppermute | solution.py:431
  485.0 38.8 %collective-permute-start.45 = (bf16[3,2,144,256]{3,2,0,1:T(8,128)(2,1)}, bf16[3,2,144,256]{3,2,0,1:T(8,128)(2,1)S(1)}, u32[]{:S(2)}, u32[]{:S(2)}) collective-permute-start(bf16[3,2,144,256]{3,2,0,1:T(8,128)(2,1)} %get-tuple-element.130), channel_id=1, source_target_pairs={{0,4},{2,6},{4,0},{6,2},{1,5},{3,7},{5,1},{7,3},{8,12},{10,14},{12... | collective-permute-start | bytes 1327112 | tf_op jit(solution)/shard_map/ppermute | solution.py:458
  485.9 41.0 %collective-permute-start.44 = (bf16[3,2,144,256]{3,2,0,1:T(8,128)(2,1)}, bf16[3,2,144,256]{3,2,0,1:T(8,128)(2,1)S(1)}, u32[]{:S(2)}, u32[]{:S(2)}) collective-permute-start(bf16[3,2,144,256]{3,2,0,1:T(8,128)(2,1)} %get-tuple-element.128), channel_id=1, source_target_pairs={{0,2},{2,0},{4,6},{6,4},{1,3},{3,1},{5,7},{7,5},{8,10},{10,8},{12,... | collective-permute-start | bytes 1327112 | tf_op jit(solution)/shard_map/ppermute | solution.py:458
  499.6 31.9 %collective-permute-start.25 = (bf16[26,1,16,512]{3,2,1,0:T(8,128)(2,1)}, bf16[26,1,16,512]{3,2,1,0:T(8,128)(2,1)S(1)}, u32[]{:S(2)}, u32[]{:S(2)}) collective-permute-start(bf16[26,1,16,512]{3,2,1,0:T(8,128)(2,1)} %get-tuple-element.131), channel_id=1, source_target_pairs={{0,1},{1,2},{2,3},{3,4},{4,5},{5,6},{6,7},{8,9},{9,10},{10,11},{11... | collective-permute-start | bytes 1277960 | tf_op jit(solution)/shard_map/ppermute | solution.py:431
  527.7 26.3 %collective-permute-start.30 = (bf16[1,4,2,144,256]{4,3,2,1,0:T(8,128)(2,1)S(1)}, bf16[1,4,2,144,256]{4,3,2,1,0:T(8,128)(2,1)S(1)}, u32[]{:S(2)}, u32[]{:S(2)}) collective-permute-start(bf16[1,4,2,144,256]{4,3,2,1,0:T(8,128)(2,1)S(1)} %get-tuple-element.127), channel_id=1, source_target_pairs={{0,16},{8,24},{16,0},{24,8},{1,17},{9,25},{17,1},{25,9},{2,18},{10... | collective-permute-start | bytes 1769480 | tf_op jit(solution)/shard_map/ppermute | solution.py:458
  593.3 47.8 %collective-permute-start.37 = (bf16[1,144,512]{2,1,0:T(8,128)(2,1)S(1)}, bf16[1,144,512]{2,1,0:T(8,128)(2,1)S(1)}, u32[]{:S(2)}, u32[]{:S(2)}) collective-permute-start(bf16[1,144,512]{2,1,0:T(8,128)(2,1)S(1)} %pad_maximum_fusion.13.refs_0_), channel_id=1, source_target_pairs={{0,16},{8,24},{16,0},{24,8},{1,17},{9,25},{17,1},{25,9},{2,18},{10... | collective-permute-start | bytes 442376 | tf_op jit(solution)/shard_map/ppermute | solution.py:458
  594.7 46.4 %collective-permute-start.38 = (bf16[1,144,512]{2,1,0:T(8,128)(2,1)S(1)}, bf16[1,144,512]{2,1,0:T(8,128)(2,1)S(1)}, u32[]{:S(2)}, u32[]{:S(2)}) collective-permute-start(bf16[1,144,512]{2,1,0:T(8,128)(2,1)S(1)} %pad_maximum_fusion.13.refs_0_), channel_id=1, source_target_pairs={{0,24},{8,16},{16,8},{24,0},{1,25},{9,17},{17,9},{25,1},{2,26},{10... | collective-permute-start | bytes 442376 | tf_op jit(solution)/shard_map/ppermute | solution.py:458
  596.0 51.6 %collective-permute-start.59 = (bf16[6,16,512]{2,1,0:T(8,128)(2,1)S(1)}, bf16[6,16,512]{2,1,0:T(8,128)(2,1)S(1)}, u32[]{:S(2)}, u32[]{:S(2)}) collective-permute-start(bf16[6,16,512]{2,1,0:T(8,128)(2,1)S(1)} %pad_maximum_fusion.14.refs_0_), channel_id=1, source_target_pairs={{0,8},{8,0},{16,24},{24,16},{1,9},{9,1},{17,25},{25,17},{2,10},{10... | collective-permute-start | bytes 294920 | tf_op jit(solution)/shard_map/ppermute | solution.py:458
  601.2 46.4 %collective-permute-start.60 = (bf16[6,16,512]{2,1,0:T(8,128)(2,1)S(1)}, bf16[6,16,512]{2,1,0:T(8,128)(2,1)S(1)}, u32[]{:S(2)}, u32[]{:S(2)}) collective-permute-start(bf16[6,16,512]{2,1,0:T(8,128)(2,1)S(1)} %pad_maximum_fusion.14.refs_0_), channel_id=1, source_target_pairs={{0,16},{8,24},{16,0},{24,8},{1,17},{9,25},{17,1},{25,9},{2,18},{10... | collective-permute-start | bytes 294920 | tf_op jit(solution)/shard_map/ppermute | solution.py:458
  606.0 41.7 %collective-permute-start.61 = (bf16[6,16,512]{2,1,0:T(8,128)(2,1)S(1)}, bf16[6,16,512]{2,1,0:T(8,128)(2,1)S(1)}, u32[]{:S(2)}, u32[]{:S(2)}) collective-permute-start(bf16[6,16,512]{2,1,0:T(8,128)(2,1)S(1)} %pad_maximum_fusion.14.refs_0_), channel_id=1, source_target_pairs={{0,24},{8,16},{16,8},{24,0},{1,25},{9,17},{17,9},{25,1},{2,26},{10... | collective-permute-start | bytes 294920 | tf_op jit(solution)/shard_map/ppermute | solution.py:458
  (88 other events, 888.8 us)
Sparse Core Ops, SparseCore 0:
  11.5 71.4 all-gather.2
  86.5 127.7 all-gather.4
